TPU v7x, 256 devices: a whole 4x4x8 slice. The times are simulated.
256 devices in a mesh: gx: 32 (over x, z), gz: 8 (over y, core).
Axes of the slice: x: 4, y: 4, z: 8, core: 2. Of those that a mesh axis runs over, the one named last changes fastest.
Arguments:
- potential: float32 [32, 2048, 2048], P('gz', 'gx'), may hold values from -6 to 6
- regions: int32 [32, 2048, 2048], P('gz', 'gx'), may hold values from 0 to 15, as said below
- charge: float32 [32, 2048, 2048], P('gz', 'gx'), may hold values from -6 to 6
- levels: float32 [16], replicated, may hold values from -2 to 2
Outputs:
- field_out: float32 [32, 2048, 2048], P('gz', 'gx')
- multipoles: float32 [32, 64], P('gz', 'gx')
Inputs may be any that keep to these rules, and one draw needn't show every extreme that they name: `regions`: about three quarters of the cells are free space (id 0); the others carry ids 1 to 15 evenly.
All inputs are finite; a program needn't handle non-finite values.
Results may differ from a plain program's by a relative error of at most 0.00026.
Values sent between devices are 32-bit elements; how exact they have to be, the bound alone decides.
No kernel may reach another device: no remote copies, remote signals or barrier semaphores. Data moves between devices by JAX's collectives and lax.ppermute only.
A program may use at most 128 MiB of HBM per device.

v0:
```python
import jax
import jax.numpy as jnp
from jax import lax
from jax.sharding import PartitionSpec as P

K = 64
SWEEPS = 4


relax_factor = 1.5


def extended(cells, sides, width):
    for axis, dim in sides:
        count = lax.axis_size(axis)
        ends = count - 1
        head = lax.slice_in_dim(cells, 0, width, axis=dim)
        tail = lax.slice_in_dim(cells, cells.shape[dim] - width, cells.shape[dim], axis=dim)
        cells = jnp.concatenate(
            [
                lax.ppermute(tail, axis, [(i, (i + 1) % count) for i in range(ends)]),
                cells,
                lax.ppermute(head, axis, [((i + 1) % count, i) for i in range(ends)]),
            ],
            axis=dim,
        )
    return cells


def parity_grid(z_start, x_start, planes, row_count, columns):
    shape = (planes, row_count, columns)
    total = (
        lax.broadcasted_iota(jnp.int32, shape, 0)
        + lax.broadcasted_iota(jnp.int32, shape, 1)
        + lax.broadcasted_iota(jnp.int32, shape, 2)
    )
    return (total + z_start + x_start + 8) % 2


def relax_cells(values, free_cells, charge_in, parity_in, colour):
    center = values[1:-1, 1:-1]
    side_pad = jnp.pad(center, ((0, 0), (0, 0), (1, 1)))
    beside = (
        values[2:, 1:-1]
        + values[:-2, 1:-1]
        + values[1:-1, 2:]
        + values[1:-1, :-2]
        + side_pad[:, :, 2:]
        + side_pad[:, :, :-2]
    )
    target = (beside + charge_in) / 6.0
    moved = center + relax_factor * (target - center)
    return jnp.where((free_cells > 0.5) & (parity_in == colour), moved, center)


def make_basis(x_start, row_count, rows_total, columns, terms):
    row_pos = (x_start + jnp.arange(row_count, dtype=jnp.int32)).astype(jnp.float32)
    col_pos = jnp.arange(columns, dtype=jnp.int32).astype(jnp.float32)
    coord_x = (row_pos + 0.5) * (2.0 / rows_total) - 1.0
    coord_y = (col_pos + 0.5) * (2.0 / columns) - 1.0
    coord_x = coord_x[:, None] + 0.0 * coord_y[None, :]
    coord_y = coord_y[None, :] + 0.0 * coord_x
    radius = jnp.sqrt(coord_x * coord_x + coord_y * coord_y)
    angle_grid = jnp.arctan2(coord_y, coord_x)
    orders = jnp.arange(1, terms // 2 + 1, dtype=jnp.int32).astype(jnp.float32)[:, None, None]
    return jnp.concatenate(
        [radius * jnp.cos(orders * angle_grid), radius * jnp.sin(orders * angle_grid)], axis=0
    )


def local(potential, regions, charge, levels):
    planes, row_count, columns = potential.shape
    z_start = lax.axis_index("gz") * planes
    x_start = lax.axis_index("gx") * row_count
    rows_total = lax.axis_size("gx") * row_count
    free_cells = (regions == 0).astype(jnp.float32)
    pinned = jnp.zeros(potential.shape, jnp.float32)
    for region in range(levels.shape[0]):
        pinned = jnp.where(regions == region, levels[region], pinned)
    field_now = jnp.where(free_cells > 0.5, potential, pinned)
    parity_in = parity_grid(z_start, x_start, planes, row_count, columns)
    for sweep_index in range(SWEEPS):
        for colour in (0, 1):
            padded = extended(field_now, (("gz", 0), ("gx", 1)), 1)
            field_now = relax_cells(padded, free_cells, charge, parity_in, colour)
    block = min(16, row_count)
    partial_terms = jnp.zeros((planes, K), jnp.float32)
    for start in range(0, row_count, block):
        basis_table = make_basis(x_start + start, block, rows_total, columns, K)
        partial_terms = partial_terms + jnp.einsum(
            "zxy,kxy->zk",
            field_now[:, start : start + block],
            basis_table,
            precision=lax.Precision.HIGHEST,
        )
    partial_terms = partial_terms * (1.0 / jnp.sqrt(jnp.float32(rows_total) * jnp.float32(columns)))
    summed = lax.psum(partial_terms, "gx")
    share = K // lax.axis_size("gx")
    multipoles = lax.dynamic_slice_in_dim(summed, lax.axis_index("gx") * share, share, 1)
    return (field_now, multipoles)


def solution(mesh):
    in_specs = (P("gz", "gx", None), P("gz", "gx", None), P("gz", "gx", None), P())
    out_specs = (P("gz", "gx", None), P("gz", "gx"))
    return jax.shard_map(local, mesh=mesh, in_specs=in_specs, out_specs=out_specs, check_vma=False)
```

profile of v0, /device:TPU:8, one launch (start us, length us, event | category | flops | bytes accessed | tf_op | source)
XLA Modules:
  0.0 560.1 jit_solution(1528851226551430376)
XLA Ops:
  0.6 2.0 fusion.149
  2.6 17.6 %copy_select_fusion = (f32[4,64,2048]{2,0,1:T(4,128)S(1)}, pred[4,64,2048]{2,0,1:T(4,128)(4,1)S(1)}) fusion(f32[4,64,2048]{2,1,0:T(8,128)} %param.4, s32[4,64,2048]{2,1,0:T(8,128)} %param.5, f32[]{:T(128)} %bitcast.15, f32[]{:T(128)} %bitcast.14, f32[]{:T(128)} %bitcast.13, f32[]{:T(128)} %bitcast.12, f32[]{:T(128)} %bitcast.11, f32[]{:T(128)} %bitcast.10, ...), kind=kLoop, calls=%fused_computation.180 | loop fusion | flops 18350080 | bytes 6815808 | tf_op jit(solution)/shard_map/jit(_where)/select_n | solution.py:80
  21.0 2.1 collective-permute-start.1
  23.1 3.6 collective-permute-start
  26.7 4.9 collective-permute-done.1
  35.5 4.5 collective-permute-start.3
  42.0 17.2 %add_select_fusion.7 = f32[4,64,2048]{2,0,1:T(4,128)S(1)} fusion(f32[4,64,2048]{2,0,1:T(4,128)} %copy-done.2, f32[6,1,2048]{2,0,1:T(8,128)S(1)} %collective-permute-done.3, f32[1,64,2048]{2,0,1:T(1,128)} %copy-done.13, f32[1,64,2048]{2,0,1:T(1,128)S(1)} %collective-permute-done.1, f32[6,1,2048]{2,0,1:T(8,128)S(1)} %collective-permute-done.2, ...), kind=kLoop, calls=%fused_computation.39 | loop fusion | flops 19398656 | bytes 7962632 | tf_op jit(solution)/shard_map/jit(_where)/select_n | solution.py:53
  60.0 2.8 collective-permute-start.5
  62.8 2.8 collective-permute-start.4
  65.5 4.9 collective-permute-done.5
  73.6 5.1 collective-permute-start.7
  80.4 12.9 %add_select_fusion.6 = f32[4,64,2048]{2,0,1:T(4,128)S(1)} fusion(f32[4,64,2048]{2,0,1:T(4,128)S(1)} %add_select_fusion.7, f32[6,1,2048]{2,0,1:T(8,128)S(1)} %collective-permute-done.7, f32[1,64,2048]{2,0,1:T(1,128)S(1)} %collective-permute-done.4, f32[1,64,2048]{2,0,1:T(1,128)S(1)} %collective-permute-done.5, f32[6,1,2048]{2,0,1:T(8,128)S(1)} %collective-permute-done.6, ...), kind=kLoop, calls=%fused_computation.38 | loop fusion | flops 19398656 | bytes 7962632 | tf_op jit(solution)/shard_map/jit(_where)/select_n | solution.py:53
  94.1 3.2 collective-permute-start.9
  97.3 2.4 collective-permute-start.8
  99.6 4.9 collective-permute-done.9
  107.7 4.9 collective-permute-start.11
  114.5 12.9 %add_select_fusion.5 = f32[4,64,2048]{2,0,1:T(4,128)S(1)} fusion(f32[4,64,2048]{2,0,1:T(4,128)S(1)} %add_select_fusion.6, f32[6,1,2048]{2,0,1:T(8,128)S(1)} %collective-permute-done.11, f32[1,64,2048]{2,0,1:T(1,128)S(1)} %collective-permute-done.8, f32[1,64,2048]{2,0,1:T(1,128)S(1)} %collective-permute-done.9, f32[6,1,2048]{2,0,1:T(8,128)S(1)} %collective-permute-done.10, ...), kind=kLoop, calls=%fused_computation.37 | loop fusion | flops 19398656 | bytes 7962632 | tf_op jit(solution)/shard_map/jit(_where)/select_n | solution.py:53
  128.2 3.6 collective-permute-start.13
  131.7 2.0 collective-permute-start.12
  133.7 4.9 collective-permute-done.13
  141.8 5.1 collective-permute-start.15
  148.5 12.9 %add_select_fusion.4 = f32[4,64,2048]{2,0,1:T(4,128)S(1)} fusion(f32[4,64,2048]{2,0,1:T(4,128)S(1)} %add_select_fusion.5, f32[6,1,2048]{2,0,1:T(8,128)S(1)} %collective-permute-done.15, f32[1,64,2048]{2,0,1:T(1,128)S(1)} %collective-permute-done.12, f32[1,64,2048]{2,0,1:T(1,128)S(1)} %collective-permute-done.13, ...), kind=kLoop, calls=%fused_computation.36 | loop fusion | flops 19398656 | bytes 7962632 | tf_op jit(solution)/shard_map/jit(_where)/select_n | solution.py:53
  162.2 4.2 collective-permute-start.17
  166.5 1.9 collective-permute-start.16
  168.4 4.4 collective-permute-done.17
  172.8 2.3 collective-permute-done.16
  176.4 5.8 %collective-permute-start.19 = (f32[6,1,2048]{2,0,1:T(8,128)S(1)}, f32[6,1,2048]{2,0,1:T(8,128)S(1)}, u32[]{:S(2)}, u32[]{:S(2)}) collective-permute-start(f32[6,1,2048]{2,0,1:T(8,128)S(1)} %get-tuple-element.13), channel_id=1, source_target_pairs={{0,8},{8,16},{16,24},{24,32},{32,40},{40,48},{48,56},{56,64},{64,7... | collective-permute-start | bytes 147464 | tf_op jit(solution)/shard_map/ppermute | solution.py:21
  184.1 12.9 %add_select_fusion.3 = f32[4,64,2048]{2,0,1:T(4,128)S(1)} fusion(f32[4,64,2048]{2,0,1:T(4,128)S(1)} %add_select_fusion.4, f32[6,1,2048]{2,0,1:T(8,128)S(1)} %collective-permute-done.19, f32[1,64,2048]{2,0,1:T(1,128)S(1)} %collective-permute-done.16, f32[1,64,2048]{2,0,1:T(1,128)S(1)} %collective-permute-done.17, ...), kind=kLoop, calls=%fused_computation.35 | loop fusion | flops 19398656 | bytes 7962632 | tf_op jit(solution)/shard_map/jit(_where)/select_n | solution.py:53
  197.8 3.7 collective-permute-start.21
  203.5 4.8 collective-permute-done.21
  211.5 6.5 %collective-permute-start.23 = (f32[6,1,2048]{2,0,1:T(8,128)S(1)}, f32[6,1,2048]{2,0,1:T(8,128)S(1)}, u32[]{:S(2)}, u32[]{:S(2)}) collective-permute-start(f32[6,1,2048]{2,0,1:T(8,128)S(1)} %get-tuple-element.11), channel_id=1, source_target_pairs={{0,8},{8,16},{16,24},{24,32},{32,40},{40,48},{48,56},{56,64},{64,7... | collective-permute-start | bytes 147464 | tf_op jit(solution)/shard_map/ppermute | solution.py:21
  219.5 12.9 %add_select_fusion.2 = f32[4,64,2048]{2,0,1:T(4,128)S(1)} fusion(f32[4,64,2048]{2,0,1:T(4,128)S(1)} %add_select_fusion.3, f32[6,1,2048]{2,0,1:T(8,128)S(1)} %collective-permute-done.23, f32[1,64,2048]{2,0,1:T(1,128)S(1)} %collective-permute-done.20, f32[1,64,2048]{2,0,1:T(1,128)S(1)} %collective-permute-done.21, ...), kind=kLoop, calls=%fused_computation.34 | loop fusion | flops 19398656 | bytes 7962632 | tf_op jit(solution)/shard_map/jit(_where)/select_n | solution.py:53
  235.5 3.6 collective-permute-start.25
  239.2 1.9 collective-permute-start.24
  241.2 5.1 collective-permute-done.25
  250.3 6.2 %collective-permute-start.27 = (f32[6,1,2048]{2,0,1:T(8,128)S(1)}, f32[6,1,2048]{2,0,1:T(8,128)S(1)}, u32[]{:S(2)}, u32[]{:S(2)}) collective-permute-start(f32[6,1,2048]{2,0,1:T(8,128)S(1)} %get-tuple-element.9), channel_id=1, source_target_pairs={{0,8},{8,16},{16,24},{24,32},{32,40},{40,48},{48,56},{56,64},{64,7... | collective-permute-start | bytes 147464 | tf_op jit(solution)/shard_map/ppermute | solution.py:21
  258.3 17.3 %add_select_fusion.1 = f32[4,64,2048]{2,0,1:T(4,128)S(1)} fusion(f32[4,64,2048]{2,0,1:T(4,128)} %copy-done.3, f32[6,1,2048]{2,0,1:T(8,128)S(1)} %collective-permute-done.27, f32[1,64,2048]{2,0,1:T(1,128)} %collective-permute-done.24, f32[1,64,2048]{2,0,1:T(1,128)S(1)} %collective-permute-done.25, f32[6,1,2048]{2,0,1:T(8,128)S(1)} %collective-permute-done.26, ...), kind=kLoop, calls=%fused_computation.33 | loop fusion | flops 19398656 | bytes 7962632 | tf_op jit(solution)/shard_map/jit(_where)/select_n | solution.py:53
  276.4 3.6 collective-permute-start.29
  283.1 3.8 collective-permute-done.29
  290.8 6.3 %collective-permute-start.31 = (f32[6,1,2048]{2,0,1:T(8,128)S(1)}, f32[6,1,2048]{2,0,1:T(8,128)S(1)}, u32[]{:S(2)}, u32[]{:S(2)}) collective-permute-start(f32[6,1,2048]{2,0,1:T(8,128)S(1)} %get-tuple-element.7), channel_id=1, source_target_pairs={{0,8},{8,16},{16,24},{24,32},{32,40},{40,48},{48,56},{56,64},{64,7... | collective-permute-start | bytes 147464 | tf_op jit(solution)/shard_map/ppermute | solution.py:21
  297.1 63.7 %fusion.16 = (f32[32,16,2048]{2,0,1:T(8,128)}, f32[32,16,2048]{2,0,1:T(8,128)}, f32[32,16,2048]{2,0,1:T(8,128)}, f32[32,16,2048]{2,0,1:T(8,128)}, f32[32,16,2048...) fusion(f32[16,2048]{1,0:T(8,128)S(1)} %get-tuple-element.47, ...), kind=kLoop, calls=%fused_computation.24 | loop fusion | flops 12582912 | bytes 34603136 | tf_op jit(solution)/shard_map/mul | solution.py:67
  360.8 17.5 %add_select_fusion = f32[4,64,2048]{2,0,1:T(4,128)S(1)} fusion(f32[4,64,2048]{2,0,1:T(4,128)} %copy-done.1, f32[6,1,2048]{2,0,1:T(8,128)S(1)} %collective-permute-done.31, f32[1,64,2048]{2,0,1:T(1,128)} %copy-done.12, f32[1,64,2048]{2,0,1:T(1,128)S(1)} %collective-permute-done.29, f32[6,1,2048]{2,0,1:T(8,128)S(1)} %collective-permute-done.30, ...), kind=kLoop, calls=%fused_computation.32 | loop fusion | flops 19398656 | bytes 7962632 | tf_op jit(solution)/shard_map/jit(_where)/select_n | solution.py:53
  378.3 2.5 copy.31
  380.9 6.6 %fusion.103 = f32[4,64]{0,1:T(8,128)S(1)} fusion(f32[4,64,2048]{2,0,1:T(4,128)S(1)} %add_select_fusion, f32[32,16,2048]{2,0,1:T(8,128)S(1)} %copy-done.10, f32[32,16,2048]{2,0,1:T(8,128)S(1)} %copy-done.11), kind=kOutput, calls=%fused_computation.187 | convolution fusion | flops 102760448 | bytes 10486784 | tf_op jit(solution)/shard_map/zxy,kxy->zk/dot_general | solution.py:90
  387.5 7.0 %fusion.100 = f32[4,64]{0,1:T(8,128)S(1)} fusion(f32[4,64,2048]{2,0,1:T(4,128)S(1)} %add_select_fusion, f32[32,16,2048]{2,0,1:T(8,128)S(1)} %copy-done.8, f32[32,16,2048]{2,0,1:T(8,128)S(1)} %copy-done.9), kind=kOutput, calls=%fused_computation.186 | convolution fusion | flops 102760448 | bytes 10486784 | tf_op jit(solution)/shard_map/zxy,kxy->zk/dot_general | solution.py:90
  394.6 6.6 %fusion.97 = f32[4,64]{0,1:T(8,128)S(1)} fusion(f32[4,64,2048]{2,0,1:T(4,128)S(1)} %add_select_fusion, f32[32,16,2048]{2,0,1:T(8,128)S(1)} %copy-done.6, f32[32,16,2048]{2,0,1:T(8,128)S(1)} %copy-done.7), kind=kOutput, calls=%fused_computation.185 | convolution fusion | flops 102760448 | bytes 10486784 | tf_op jit(solution)/shard_map/zxy,kxy->zk/dot_general | solution.py:90
  401.2 7.0 %fusion.118 = f32[4,64]{0,1:T(8,128)S(1)} fusion(f32[4,64]{0,1:T(8,128)S(1)} %fusion.97, f32[4,64]{0,1:T(8,128)S(1)} %fusion.100, f32[4,64]{0,1:T(8,128)S(1)} %fusion.103, f32[4,64,2048]{2,0,1:T(4,128)S(1)} %add_select_fusion, f32[32,16,2048]{2,0,1:T(8,128)S(1)} %copy-done.5, f32[32,16,2048]{2,0,1:T(8,128)S(1)} %copy-done.4), kind=kOutput, calls=%fused_computation.192 | convolution fusion | flops 102761472 | bytes 10489856 | tf_op jit(solution)/shard_map/zxy,kxy->zk/dot_general | solution.py:90
  408.3 151.1 %psum.7 = f32[4,64]{0,1:T(8,128)S(1)} all-reduce(f32[4,64]{0,1:T(8,128)S(1)} %fusion.118), channel_id=1, replica_groups=mesh['gx'=32,'gz'=8] {'gx'}, use_global_device_ids=true, to_apply=%region_0.1 | all-reduce | flops 256 | bytes 2048 | tf_op jit(solution)/shard_map/psum | solution.py:97
  (84 shorter events, 52.2 us)
Async XLA Ops:
  20.2 13.3 %copy-start.2 = (f32[4,64,2048]{2,0,1:T(4,128)}, f32[4,64,2048]{2,0,1:T(4,128)S(1)}, u32[]{:S(2)}) copy-start(f32[4,64,2048]{2,0,1:T(4,128)S(1)} %get-tuple-element.4) | copy-start | bytes 6291460
  21.0 20.9 %copy-start = (f32[4,64,2048]{2,1,0:T(8,128)S(1)}, f32[4,64,2048]{2,1,0:T(8,128)}, u32[]{:S(2)}) copy-start(f32[4,64,2048]{2,1,0:T(8,128)} %param.6) | copy-start | bytes 6291460
  21.0 10.6 %collective-permute-start.1 = (f32[1,64,2048]{2,0,1:T(1,128)S(1)}, f32[1,64,2048]{2,0,1:T(1,128)S(1)}, u32[]{:S(2)}, u32[]{:S(2)}) collective-permute-start(f32[1,64,2048]{2,0,1:T(1,128)S(1)} %get-tuple-element.36), channel_id=1, source_target_pairs={{0,1},{1,2},{2,3},{3,4},{4,5},{5,6},{6,7},{8,9},{9,10},{10,11},{11... | collective-permute-start | bytes 1572872 | tf_op jit(solution)/shard_map/ppermute | solution.py:21
  23.1 10.3 %collective-permute-start = (f32[1,64,2048]{2,0,1:T(1,128)S(1)}, f32[1,64,2048]{2,0,1:T(1,128)S(1)}, u32[]{:S(2)}, u32[]{:S(2)}) collective-permute-start(f32[1,64,2048]{2,0,1:T(1,128)S(1)} %get-tuple-element.37), channel_id=1, source_target_pairs={{1,0},{2,1},{3,2},{4,3},{5,4},{6,5},{7,6},{9,8},{10,9},{11,10},{12... | collective-permute-start | bytes 1572872 | tf_op jit(solution)/shard_map/ppermute | solution.py:23
  33.4 0.8 copy-start.13
  34.2 6.1 %collective-permute-start.2 = (f32[6,1,2048]{2,0,1:T(8,128)S(1)}, f32[6,1,2048]{2,0,1:T(8,128)S(1)}, u32[]{:S(2)}, u32[]{:S(2)}) collective-permute-start(f32[6,1,2048]{2,0,1:T(8,128)S(1)} %get-tuple-element.20), channel_id=1, source_target_pairs={{8,0},{16,8},{24,16},{32,24},{40,32},{48,40},{56,48},{64,56},{72,6... | collective-permute-start | bytes 147464 | tf_op jit(solution)/shard_map/ppermute | solution.py:23
  35.5 6.4 %collective-permute-start.3 = (f32[6,1,2048]{2,0,1:T(8,128)S(1)}, f32[6,1,2048]{2,0,1:T(8,128)S(1)}, u32[]{:S(2)}, u32[]{:S(2)}) collective-permute-start(f32[6,1,2048]{2,0,1:T(8,128)S(1)} %get-tuple-element.21), channel_id=1, source_target_pairs={{0,8},{8,16},{16,24},{24,32},{32,40},{40,48},{48,56},{56,64},{64,7... | collective-permute-start | bytes 147464 | tf_op jit(solution)/shard_map/ppermute | solution.py:21
  60.0 10.5 %collective-permute-start.5 = (f32[1,64,2048]{2,0,1:T(1,128)S(1)}, f32[1,64,2048]{2,0,1:T(1,128)S(1)}, u32[]{:S(2)}, u32[]{:S(2)}) collective-permute-start(f32[1,64,2048]{2,0,1:T(1,128)S(1)} %get-tuple-element.34), channel_id=1, source_target_pairs={{0,1},{1,2},{2,3},{3,4},{4,5},{5,6},{6,7},{8,9},{9,10},{10,11},{11... | collective-permute-start | bytes 1572872 | tf_op jit(solution)/shard_map/ppermute | solution.py:21
  62.8 9.4 %collective-permute-start.4 = (f32[1,64,2048]{2,0,1:T(1,128)S(1)}, f32[1,64,2048]{2,0,1:T(1,128)S(1)}, u32[]{:S(2)}, u32[]{:S(2)}) collective-permute-start(f32[1,64,2048]{2,0,1:T(1,128)S(1)} %get-tuple-element.35), channel_id=1, source_target_pairs={{1,0},{2,1},{3,2},{4,3},{5,4},{6,5},{7,6},{9,8},{10,9},{11,10},{12... | collective-permute-start | bytes 1572872 | tf_op jit(solution)/shard_map/ppermute | solution.py:23
  72.3 6.5 %collective-permute-start.6 = (f32[6,1,2048]{2,0,1:T(8,128)S(1)}, f32[6,1,2048]{2,0,1:T(8,128)S(1)}, u32[]{:S(2)}, u32[]{:S(2)}) collective-permute-start(f32[6,1,2048]{2,0,1:T(8,128)S(1)} %get-tuple-element.18), channel_id=1, source_target_pairs={{8,0},{16,8},{24,16},{32,24},{40,32},{48,40},{56,48},{64,56},{72,6... | collective-permute-start | bytes 147464 | tf_op jit(solution)/shard_map/ppermute | solution.py:23
  73.6 6.8 %collective-permute-start.7 = (f32[6,1,2048]{2,0,1:T(8,128)S(1)}, f32[6,1,2048]{2,0,1:T(8,128)S(1)}, u32[]{:S(2)}, u32[]{:S(2)}) collective-permute-start(f32[6,1,2048]{2,0,1:T(8,128)S(1)} %get-tuple-element.19), channel_id=1, source_target_pairs={{0,8},{8,16},{16,24},{24,32},{32,40},{40,48},{48,56},{56,64},{64,7... | collective-permute-start | bytes 147464 | tf_op jit(solution)/shard_map/ppermute | solution.py:21
  94.1 10.5 %collective-permute-start.9 = (f32[1,64,2048]{2,0,1:T(1,128)S(1)}, f32[1,64,2048]{2,0,1:T(1,128)S(1)}, u32[]{:S(2)}, u32[]{:S(2)}) collective-permute-start(f32[1,64,2048]{2,0,1:T(1,128)S(1)} %get-tuple-element.32), channel_id=1, source_target_pairs={{0,1},{1,2},{2,3},{3,4},{4,5},{5,6},{6,7},{8,9},{9,10},{10,11},{11... | collective-permute-start | bytes 1572872 | tf_op jit(solution)/shard_map/ppermute | solution.py:21
  97.3 9.1 %collective-permute-start.8 = (f32[1,64,2048]{2,0,1:T(1,128)S(1)}, f32[1,64,2048]{2,0,1:T(1,128)S(1)}, u32[]{:S(2)}, u32[]{:S(2)}) collective-permute-start(f32[1,64,2048]{2,0,1:T(1,128)S(1)} %get-tuple-element.33), channel_id=1, source_target_pairs={{1,0},{2,1},{3,2},{4,3},{5,4},{6,5},{7,6},{9,8},{10,9},{11,10},{12... | collective-permute-start | bytes 1572872 | tf_op jit(solution)/shard_map/ppermute | solution.py:23
  106.4 6.5 %collective-permute-start.10 = (f32[6,1,2048]{2,0,1:T(8,128)S(1)}, f32[6,1,2048]{2,0,1:T(8,128)S(1)}, u32[]{:S(2)}, u32[]{:S(2)}) collective-permute-start(f32[6,1,2048]{2,0,1:T(8,128)S(1)} %get-tuple-element.16), channel_id=1, source_target_pairs={{8,0},{16,8},{24,16},{32,24},{40,32},{48,40},{56,48},{64,56},{72,6... | collective-permute-start | bytes 147464 | tf_op jit(solution)/shard_map/ppermute | solution.py:23
  107.7 6.8 %collective-permute-start.11 = (f32[6,1,2048]{2,0,1:T(8,128)S(1)}, f32[6,1,2048]{2,0,1:T(8,128)S(1)}, u32[]{:S(2)}, u32[]{:S(2)}) collective-permute-start(f32[6,1,2048]{2,0,1:T(8,128)S(1)} %get-tuple-element.17), channel_id=1, source_target_pairs={{0,8},{8,16},{16,24},{24,32},{32,40},{40,48},{48,56},{56,64},{64,7... | collective-permute-start | bytes 147464 | tf_op jit(solution)/shard_map/ppermute | solution.py:21
  128.2 10.5 %collective-permute-start.13 = (f32[1,64,2048]{2,0,1:T(1,128)S(1)}, f32[1,64,2048]{2,0,1:T(1,128)S(1)}, u32[]{:S(2)}, u32[]{:S(2)}) collective-permute-start(f32[1,64,2048]{2,0,1:T(1,128)S(1)} %get-tuple-element.30), channel_id=1, source_target_pairs={{0,1},{1,2},{2,3},{3,4},{4,5},{5,6},{6,7},{8,9},{9,10},{10,11},{11... | collective-permute-start | bytes 1572872 | tf_op jit(solution)/shard_map/ppermute | solution.py:21
  131.7 8.7 %collective-permute-start.12 = (f32[1,64,2048]{2,0,1:T(1,128)S(1)}, f32[1,64,2048]{2,0,1:T(1,128)S(1)}, u32[]{:S(2)}, u32[]{:S(2)}) collective-permute-start(f32[1,64,2048]{2,0,1:T(1,128)S(1)} %get-tuple-element.31), channel_id=1, source_target_pairs={{1,0},{2,1},{3,2},{4,3},{5,4},{6,5},{7,6},{9,8},{10,9},{11,10},{12... | collective-permute-start | bytes 1572872 | tf_op jit(solution)/shard_map/ppermute | solution.py:23
  140.5 6.5 %collective-permute-start.14 = (f32[6,1,2048]{2,0,1:T(8,128)S(1)}, f32[6,1,2048]{2,0,1:T(8,128)S(1)}, u32[]{:S(2)}, u32[]{:S(2)}) collective-permute-start(f32[6,1,2048]{2,0,1:T(8,128)S(1)} %get-tuple-element.14), channel_id=1, source_target_pairs={{8,0},{16,8},{24,16},{32,24},{40,32},{48,40},{56,48},{64,56},{72,6... | collective-permute-start | bytes 147464 | tf_op jit(solution)/shard_map/ppermute | solution.py:23
  141.8 6.8 %collective-permute-start.15 = (f32[6,1,2048]{2,0,1:T(8,128)S(1)}, f32[6,1,2048]{2,0,1:T(8,128)S(1)}, u32[]{:S(2)}, u32[]{:S(2)}) collective-permute-start(f32[6,1,2048]{2,0,1:T(8,128)S(1)} %get-tuple-element.15), channel_id=1, source_target_pairs={{0,8},{8,16},{16,24},{24,32},{32,40},{40,48},{48,56},{56,64},{64,7... | collective-permute-start | bytes 147464 | tf_op jit(solution)/shard_map/ppermute | solution.py:21
  162.2 10.5 %collective-permute-start.17 = (f32[1,64,2048]{2,0,1:T(1,128)S(1)}, f32[1,64,2048]{2,0,1:T(1,128)S(1)}, u32[]{:S(2)}, u32[]{:S(2)}) collective-permute-start(f32[1,64,2048]{2,0,1:T(1,128)S(1)} %get-tuple-element.28), channel_id=1, source_target_pairs={{0,1},{1,2},{2,3},{3,4},{4,5},{5,6},{6,7},{8,9},{9,10},{10,11},{11... | collective-permute-start | bytes 1572872 | tf_op jit(solution)/shard_map/ppermute | solution.py:21
  166.5 8.6 %collective-permute-start.16 = (f32[1,64,2048]{2,0,1:T(1,128)S(1)}, f32[1,64,2048]{2,0,1:T(1,128)S(1)}, u32[]{:S(2)}, u32[]{:S(2)}) collective-permute-start(f32[1,64,2048]{2,0,1:T(1,128)S(1)} %get-tuple-element.29), channel_id=1, source_target_pairs={{1,0},{2,1},{3,2},{4,3},{5,4},{6,5},{7,6},{9,8},{10,9},{11,10},{12... | collective-permute-start | bytes 1572872 | tf_op jit(solution)/shard_map/ppermute | solution.py:23
  175.1 7.4 %collective-permute-start.18 = (f32[6,1,2048]{2,0,1:T(8,128)S(1)}, f32[6,1,2048]{2,0,1:T(8,128)S(1)}, u32[]{:S(2)}, u32[]{:S(2)}) collective-permute-start(f32[6,1,2048]{2,0,1:T(8,128)S(1)} %get-tuple-element.12), channel_id=1, source_target_pairs={{8,0},{16,8},{24,16},{32,24},{40,32},{48,40},{56,48},{64,56},{72,6... | collective-permute-start | bytes 147464 | tf_op jit(solution)/shard_map/ppermute | solution.py:23
  176.4 7.7 %collective-permute-start.19 = (f32[6,1,2048]{2,0,1:T(8,128)S(1)}, f32[6,1,2048]{2,0,1:T(8,128)S(1)}, u32[]{:S(2)}, u32[]{:S(2)}) collective-permute-start(f32[6,1,2048]{2,0,1:T(8,128)S(1)} %get-tuple-element.13), channel_id=1, source_target_pairs={{0,8},{8,16},{16,24},{24,32},{32,40},{40,48},{48,56},{56,64},{64,7... | collective-permute-start | bytes 147464 | tf_op jit(solution)/shard_map/ppermute | solution.py:21
  197.8 10.5 %collective-permute-start.21 = (f32[1,64,2048]{2,0,1:T(1,128)S(1)}, f32[1,64,2048]{2,0,1:T(1,128)S(1)}, u32[]{:S(2)}, u32[]{:S(2)}) collective-permute-start(f32[1,64,2048]{2,0,1:T(1,128)S(1)} %get-tuple-element.26), channel_id=1, source_target_pairs={{0,1},{1,2},{2,3},{3,4},{4,5},{5,6},{6,7},{8,9},{9,10},{10,11},{11... | collective-permute-start | bytes 1572872 | tf_op jit(solution)/shard_map/ppermute | solution.py:21
  201.5 8.6 %collective-permute-start.20 = (f32[1,64,2048]{2,0,1:T(1,128)S(1)}, f32[1,64,2048]{2,0,1:T(1,128)S(1)}, u32[]{:S(2)}, u32[]{:S(2)}) collective-permute-start(f32[1,64,2048]{2,0,1:T(1,128)S(1)} %get-tuple-element.27), channel_id=1, source_target_pairs={{1,0},{2,1},{3,2},{4,3},{5,4},{6,5},{7,6},{9,8},{10,9},{11,10},{12... | collective-permute-start | bytes 1572872 | tf_op jit(solution)/shard_map/ppermute | solution.py:23
  210.2 7.8 %collective-permute-start.22 = (f32[6,1,2048]{2,0,1:T(8,128)S(1)}, f32[6,1,2048]{2,0,1:T(8,128)S(1)}, u32[]{:S(2)}, u32[]{:S(2)}) collective-permute-start(f32[6,1,2048]{2,0,1:T(8,128)S(1)} %get-tuple-element.10), channel_id=1, source_target_pairs={{8,0},{16,8},{24,16},{32,24},{40,32},{48,40},{56,48},{64,56},{72,6... | collective-permute-start | bytes 147464 | tf_op jit(solution)/shard_map/ppermute | solution.py:23
  211.5 8.0 %collective-permute-start.23 = (f32[6,1,2048]{2,0,1:T(8,128)S(1)}, f32[6,1,2048]{2,0,1:T(8,128)S(1)}, u32[]{:S(2)}, u32[]{:S(2)}) collective-permute-start(f32[6,1,2048]{2,0,1:T(8,128)S(1)} %get-tuple-element.11), channel_id=1, source_target_pairs={{0,8},{8,16},{16,24},{24,32},{32,40},{40,48},{48,56},{56,64},{64,7... | collective-permute-start | bytes 147464 | tf_op jit(solution)/shard_map/ppermute | solution.py:21
  232.4 1.3 copy-start.3
  235.5 10.7 %collective-permute-start.25 = (f32[1,64,2048]{2,0,1:T(1,128)}, f32[1,64,2048]{2,0,1:T(1,128)S(1)}, u32[]{:S(2)}, u32[]{:S(2)}) collective-permute-start(f32[1,64,2048]{2,0,1:T(1,128)} %get-tuple-element.24), channel_id=1, source_target_pairs={{0,1},{1,2},{2,3},{3,4},{4,5},{5,6},{6,7},{8,9},{9,10},{10,11},{11... | collective-permute-start | bytes 1572872 | tf_op jit(solution)/shard_map/ppermute | solution.py:21
  239.2 8.9 %collective-permute-start.24 = (f32[1,64,2048]{2,0,1:T(1,128)}, f32[1,64,2048]{2,0,1:T(1,128)}, u32[]{:S(2)}, u32[]{:S(2)}) collective-permute-start(f32[1,64,2048]{2,0,1:T(1,128)} %get-tuple-element.25), channel_id=1, source_target_pairs={{1,0},{2,1},{3,2},{4,3},{5,4},{6,5},{7,6},{9,8},{10,9},{11,10},{12... | collective-permute-start | bytes 1572872 | tf_op jit(solution)/shard_map/ppermute | solution.py:23
  249.0 7.8 %collective-permute-start.26 = (f32[6,1,2048]{2,0,1:T(8,128)S(1)}, f32[6,1,2048]{2,0,1:T(8,128)S(1)}, u32[]{:S(2)}, u32[]{:S(2)}) collective-permute-start(f32[6,1,2048]{2,0,1:T(8,128)S(1)} %get-tuple-element.8), channel_id=1, source_target_pairs={{8,0},{16,8},{24,16},{32,24},{40,32},{48,40},{56,48},{64,56},{72,6... | collective-permute-start | bytes 147464 | tf_op jit(solution)/shard_map/ppermute | solution.py:23
  250.3 8.1 %collective-permute-start.27 = (f32[6,1,2048]{2,0,1:T(8,128)S(1)}, f32[6,1,2048]{2,0,1:T(8,128)S(1)}, u32[]{:S(2)}, u32[]{:S(2)}) collective-permute-start(f32[6,1,2048]{2,0,1:T(8,128)S(1)} %get-tuple-element.9), channel_id=1, source_target_pairs={{0,8},{8,16},{16,24},{24,32},{32,40},{40,48},{48,56},{56,64},{64,7... | collective-permute-start | bytes 147464 | tf_op jit(solution)/shard_map/ppermute | solution.py:21
  275.6 13.1 %copy-start.1 = (f32[4,64,2048]{2,0,1:T(4,128)}, f32[4,64,2048]{2,0,1:T(4,128)S(1)}, u32[]{:S(2)}) copy-start(f32[4,64,2048]{2,0,1:T(4,128)S(1)} %add_select_fusion.1) | copy-start | bytes 6291460
  276.4 10.5 %collective-permute-start.29 = (f32[1,64,2048]{2,0,1:T(1,128)S(1)}, f32[1,64,2048]{2,0,1:T(1,128)S(1)}, u32[]{:S(2)}, u32[]{:S(2)}) collective-permute-start(f32[1,64,2048]{2,0,1:T(1,128)S(1)} %get-tuple-element.22), channel_id=1, source_target_pairs={{0,1},{1,2},{2,3},{3,4},{4,5},{5,6},{6,7},{8,9},{9,10},{10,11},{11... | collective-permute-start | bytes 1572872 | tf_op jit(solution)/shard_map/ppermute | solution.py:21
  280.1 8.6 %collective-permute-start.28 = (f32[1,64,2048]{2,0,1:T(1,128)S(1)}, f32[1,64,2048]{2,0,1:T(1,128)S(1)}, u32[]{:S(2)}, u32[]{:S(2)}) collective-permute-start(f32[1,64,2048]{2,0,1:T(1,128)S(1)} %get-tuple-element.23), channel_id=1, source_target_pairs={{1,0},{2,1},{3,2},{4,3},{5,4},{6,5},{7,6},{9,8},{10,9},{11,10},{12... | collective-permute-start | bytes 1572872 | tf_op jit(solution)/shard_map/ppermute | solution.py:23
  288.7 0.8 copy-start.12
  289.5 71.3 %collective-permute-start.30 = (f32[6,1,2048]{2,0,1:T(8,128)S(1)}, f32[6,1,2048]{2,0,1:T(8,128)S(1)}, u32[]{:S(2)}, u32[]{:S(2)}) collective-permute-start(f32[6,1,2048]{2,0,1:T(8,128)S(1)} %get-tuple-element.6), channel_id=1, source_target_pairs={{8,0},{16,8},{24,16},{32,24},{40,32},{48,40},{56,48},{64,56},{72,6... | collective-permute-start | bytes 147464 | tf_op jit(solution)/shard_map/ppermute | solution.py:23
  290.8 70.0 %collective-permute-start.31 = (f32[6,1,2048]{2,0,1:T(8,128)S(1)}, f32[6,1,2048]{2,0,1:T(8,128)S(1)}, u32[]{:S(2)}, u32[]{:S(2)}) collective-permute-start(f32[6,1,2048]{2,0,1:T(8,128)S(1)} %get-tuple-element.7), channel_id=1, source_target_pairs={{0,8},{8,16},{16,24},{24,32},{32,40},{40,48},{48,56},{56,64},{64,7... | collective-permute-start | bytes 147464 | tf_op jit(solution)/shard_map/ppermute | solution.py:21
  360.8 20.0 %copy-start.11 = (f32[32,16,2048]{2,0,1:T(8,128)S(1)}, f32[32,16,2048]{2,0,1:T(8,128)}, u32[]{:S(2)}) copy-start(f32[32,16,2048]{2,0,1:T(8,128)} %get-tuple-element.61) | copy-start | bytes 12582916
  378.3 2.6 copy-start.10
  380.9 6.6 %copy-start.8 = (f32[32,16,2048]{2,0,1:T(8,128)S(1)}, f32[32,16,2048]{2,0,1:T(8,128)}, u32[]{:S(2)}) copy-start(f32[32,16,2048]{2,0,1:T(8,128)} %get-tuple-element.62) | copy-start | bytes 12582916
  380.9 6.6 %copy-start.9 = (f32[32,16,2048]{2,0,1:T(8,128)S(1)}, f32[32,16,2048]{2,0,1:T(8,128)}, u32[]{:S(2)}) copy-start(f32[32,16,2048]{2,0,1:T(8,128)} %get-tuple-element.63) | copy-start | bytes 12582916
  387.5 7.1 %copy-start.6 = (f32[32,16,2048]{2,0,1:T(8,128)S(1)}, f32[32,16,2048]{2,0,1:T(8,128)}, u32[]{:S(2)}) copy-start(f32[32,16,2048]{2,0,1:T(8,128)} %get-tuple-element.64) | copy-start | bytes 12582916
  387.5 7.1 %copy-start.7 = (f32[32,16,2048]{2,0,1:T(8,128)S(1)}, f32[32,16,2048]{2,0,1:T(8,128)}, u32[]{:S(2)}) copy-start(f32[32,16,2048]{2,0,1:T(8,128)} %get-tuple-element.65) | copy-start | bytes 12582916
  394.6 6.6 %copy-start.4 = (f32[32,16,2048]{2,0,1:T(8,128)S(1)}, f32[32,16,2048]{2,0,1:T(8,128)}, u32[]{:S(2)}) copy-start(f32[32,16,2048]{2,0,1:T(8,128)} %get-tuple-element.38) | copy-start | bytes 12582916
  394.6 6.6 %copy-start.5 = (f32[32,16,2048]{2,0,1:T(8,128)S(1)}, f32[32,16,2048]{2,0,1:T(8,128)}, u32[]{:S(2)}) copy-start(f32[32,16,2048]{2,0,1:T(8,128)} %get-tuple-element.39) | copy-start | bytes 12582916
where the time goes:
time: 569 us; the launch traced here: 560 us
  other arithmetic  200 us (35%)
  blocking collectives  151 us (27%)
  starting transfers between devices  100 us (18%)
  waiting for transfers between devices  65 us (11%)
  matrix products  27.3 us (5%)
  local copies, waits for them, and re-layouts  15.4 us (3%)
    psum x1, blocking collectives, local(): summed = lax.psum(partial_terms, 'gx')  151 us
    select_n x8, other arithmetic, relax_cells(): return jnp.where((free_cells > 0.5) & (parity_in == colour), moved, center)  116 us
    ppermute x16, starting transfers between devices, extended(): lax.ppermute(tail, axis, [(i, (i + 1) % count) for i in range(ends)])  71.2 us
    mul x1, other arithmetic, make_basis(): radius * jnp.cos(orders * angle_grid)  63.7 us
    ppermute x16, waiting for transfers between devices, extended(): lax.ppermute(tail, axis, [(i, (i + 1) % count) for i in range(ends)])  48.8 us
    ppermute x16, starting transfers between devices, extended(): lax.ppermute(head, axis, [((i + 1) % count, i) for i in range(ends)])  28.8 us
    dot_general x4, matrix products, local(): jnp.einsum('zxy,kxy->zk', field_now[:, start:start + block], basis_table,...  27.3 us
    select_n x1, other arithmetic, local(): field_now = jnp.where(free_cells > 0.5, potential, pinned)  17.6 us
  transfers between devices with their start and end apart: 32, of which 29 were waited for; matrix products, arithmetic and copies ran while one was open for 12% of the time, Pallas kernels for 0%

commit v1 on v0

v1 whole, which is shorter than its diff:
```python
import functools

import jax
import jax.numpy as jnp
from jax import lax
from jax.experimental import pallas as pl
from jax.experimental.pallas import tpu as pltpu
from jax.sharding import PartitionSpec as P

K = 64
SWEEPS = 4
HALF = K // 2
PINNED = 1e30
VMEM_BYTES = 40 * 1024 * 1024


def vmem():
    return pl.BlockSpec(memory_space=pltpu.VMEM)


def smem():
    return pl.BlockSpec(memory_space=pltpu.SMEM)


def column_parity(rows, columns):
    return lax.broadcasted_iota(jnp.int32, (rows, columns), 1) % 2


def pack_kernel(pot_ref, reg_ref, chg_ref, lev_ref, f0_ref, f1_ref, c0_ref, c1_ref, field, charge):
    plane = pl.program_id(0)
    rows, columns = f0_ref.shape[1:]
    table = jnp.broadcast_to(lev_ref[...], (8, 128))
    even = column_parity(rows, 128) == plane % 2
    for c in range(columns // 128):
        at = pl.ds(128 * c, 128)
        for j in range(0, 2 * rows, 8):
            to = pl.ds(j, 8)
            region = reg_ref[0, to, at]
            pinned = jnp.take_along_axis(table, region, axis=1)
            free = region == 0
            field[c, to, :] = jnp.where(free, pot_ref[0, to, at], pinned)
            charge[c, to, :] = jnp.where(free, chg_ref[0, to, at], PINNED)
        for source, out0, out1 in ((field, f0_ref, f1_ref), (charge, c0_ref, c1_ref)):
            a = source[c, pl.ds(0, rows, stride=2), :]
            b = source[c, pl.ds(1, rows, stride=2), :]
            out0[0, :, at] = jnp.where(even, a, b)
            out1[0, :, at] = jnp.where(even, b, a)


def pack(potential, regions, charge, levels):
    planes, rows, columns = potential.shape
    table = jnp.pad(levels, (0, 128 - levels.shape[0]))[None, :]
    whole = pl.BlockSpec((1, rows, columns), lambda z: (z, 0, 0))
    half = pl.BlockSpec((1, rows // 2, columns), lambda z: (z, 0, 0))
    out = jax.ShapeDtypeStruct((planes, rows // 2, columns), jnp.float32)
    return pl.pallas_call(
        pack_kernel,
        grid=(planes,),
        in_specs=[whole, whole, whole, pl.BlockSpec((1, 128), lambda z: (0, 0))],
        out_specs=[half] * 4,
        out_shape=[out] * 4,
        scratch_shapes=[pltpu.VMEM((columns // 128, rows, 128), jnp.float32)] * 2,
        compiler_params=pltpu.CompilerParams(vmem_limit_bytes=VMEM_BYTES),
        name="pack",
    )(potential, regions, charge, table)


def merge_rows(top, planes, columns, keep):
    mask = column_parity(1, columns) == keep
    return jnp.concatenate([jnp.where(mask, top[z], top[z + 1]) for z in range(0, planes, 2)], axis=0)


def sends(read, planes, rows, columns, colour, core, odd, ze_ref, zi_ref, xe_ref, xo_ref):
    for j in range(0, rows, 8):
        low, high = read(0, j, 8), read(planes - 1, j, 8)
        ze_ref[pl.ds(j, 8), :] = jnp.where(core == 0, low, high)
        zi_ref[pl.ds(j, 8), :] = jnp.where(core == 0, high, low)
    last = [read(z, rows - 1, 1) for z in range(planes)]
    first = [read(z, 0, 1) for z in range(planes)]
    above = merge_rows(last, planes, columns, 1 - colour)
    below = merge_rows(first, planes, columns, colour)
    xe_ref[...] = jnp.where(odd == 0, above, below)
    xo_ref[...] = jnp.where(odd == 0, below, above)


def relax(where, own_ref, other_ref, charge_ref, ze_ref, zi_ref, xe_ref, xo_ref, colour, put):
    core, odd = where[0], where[1]
    ze_live, below_live, above_live = where[2], where[3], where[4]
    planes, rows, columns = own_ref.shape
    column = lax.broadcasted_iota(jnp.int32, (8, columns), 1)
    row = lax.broadcasted_iota(jnp.int32, (8, columns), 0)
    xe, xo = xe_ref[...], xo_ref[...]
    below = jnp.where(below_live == 1, jnp.where(odd == 0, xo, xe), 0.0)
    above = jnp.where(above_live == 1, jnp.where(odd == 0, xe, xo), 0.0)

    def outer(j):
        far = jnp.where(ze_live == 1, ze_ref[pl.ds(j, 8), :], 0.0)
        return far, zi_ref[pl.ds(j, 8), :]

    for z in range(planes):
        first_row = (column % 2) == (z + colour) % 2
        for j in range(0, rows, 8):
            at = pl.ds(j, 8)
            mid = other_ref[z, at, :]
            if z == 0:
                far, near = outer(j)
                z_low = jnp.where(core == 0, far, near)
            else:
                z_low = other_ref[z - 1, at, :]
            if z == planes - 1:
                far, near = outer(j)
                z_high = jnp.where(core == 0, near, far)
            else:
                z_high = other_ref[z + 1, at, :]
            edge_low = below[z // 2 : z // 2 + 1] if j == 0 else other_ref[z, pl.ds(j - 1, 1), :]
            edge_high = above[z // 2 : z // 2 + 1] if j + 8 == rows else other_ref[z, pl.ds(j + 8, 1), :]
            x_low = jnp.where(row == 0, jnp.broadcast_to(edge_low, mid.shape), pltpu.roll(mid, 1, 0))
            x_high = jnp.where(row == 7, jnp.broadcast_to(edge_high, mid.shape), pltpu.roll(mid, 7, 0))
            y_low = jnp.where(column == 0, 0.0, pltpu.roll(mid, 1, 1))
            y_high = jnp.where(column == columns - 1, 0.0, pltpu.roll(mid, columns - 1, 1))
            charge = charge_ref[z, at, :]
            beside = z_low + z_high + mid + jnp.where(first_row, x_low, x_high) + y_low + y_high
            own = own_ref[z, at, :]
            put(z, j, jnp.where(charge < PINNED, 0.25 * (beside + charge) - 0.5 * own, own))


def first_send_kernel(colour, where, field_ref, ze_out, zi_out, xe_out, xo_out):
    planes, rows, columns = field_ref.shape
    sends(lambda z, j, n: field_ref[z, pl.ds(j, n), :], planes, rows, columns, colour, where[0], where[1],
          ze_out, zi_out, xe_out, xo_out)


def relax_kernel(colour, where, own_ref, other_ref, charge_ref, ze_ref, zi_ref, xe_ref, xo_ref,
                 out_ref, ze_out, zi_out, xe_out, xo_out):
    planes, rows, columns = own_ref.shape

    def put(z, j, value):
        out_ref[z, pl.ds(j, 8), :] = value

    relax(where, own_ref, other_ref, charge_ref, ze_ref, zi_ref, xe_ref, xo_ref, colour, put)
    sends(lambda z, j, n: out_ref[z, pl.ds(j, n), :], planes, rows, columns, colour, where[0], where[1],
          ze_out, zi_out, xe_out, xo_out)


def last_kernel(where, own_ref, other_ref, charge_ref, ze_ref, zi_ref, xe_ref, xo_ref, field_ref, rows_ref):
    columns = own_ref.shape[2]

    def put(z, j, value):
        even = column_parity(8, columns) == z % 2
        zero = other_ref[z, pl.ds(j, 8), :]
        low, high = jnp.where(even, zero, value), jnp.where(even, value, zero)
        for c in range(columns // 128):
            at = slice(128 * c, 128 * c + 128)
            rows_ref[z, c, pl.ds(2 * j, 8, stride=2), :] = low[:, at]
            rows_ref[z, c, pl.ds(2 * j + 1, 8, stride=2), :] = high[:, at]
            field_ref[z, pl.ds(2 * j, 16), pl.ds(128 * c, 128)] = rows_ref[z, c, pl.ds(2 * j, 16), :]

    relax(where, own_ref, other_ref, charge_ref, ze_ref, zi_ref, xe_ref, xo_ref, 1, put)


def params():
    return pltpu.CompilerParams(vmem_limit_bytes=VMEM_BYTES)


def send_shapes(planes, rows, columns):
    side = jax.ShapeDtypeStruct((rows, columns), jnp.float32)
    line = jax.ShapeDtypeStruct((planes // 2, columns), jnp.float32)
    return [side, side, line, line]


def first_send(where, field, colour):
    return pl.pallas_call(
        functools.partial(first_send_kernel, colour),
        in_specs=[smem(), vmem()],
        out_specs=[vmem()] * 4,
        out_shape=send_shapes(*field.shape),
        compiler_params=params(),
        name="first_send",
    )(where, field)


def half_sweep(where, own, other, charge, halos, colour):
    return pl.pallas_call(
        functools.partial(relax_kernel, colour),
        in_specs=[smem()] + [vmem()] * 7,
        out_specs=[vmem()] * 5,
        out_shape=[jax.ShapeDtypeStruct(own.shape, jnp.float32)] + send_shapes(*own.shape),
        compiler_params=params(),
        name="relax",
    )(where, own, other, charge, *halos)


def last_half_sweep(where, own, other, charge, halos):
    planes, rows, columns = own.shape
    return pl.pallas_call(
        last_kernel,
        in_specs=[smem()] + [vmem()] * 7,
        out_specs=vmem(),
        out_shape=jax.ShapeDtypeStruct((planes, 2 * rows, columns), jnp.float32),
        scratch_shapes=[pltpu.VMEM((planes, columns // 128, 2 * rows, 128), jnp.float32)],
        compiler_params=params(),
        name="relax_last",
    )(where, own, other, charge, *halos)


def split(value):
    high = value.astype(jnp.bfloat16)
    return high, (value - high.astype(jnp.float32)).astype(jnp.bfloat16)


def multipole_kernel(rows_total, start_ref, field_ref, out_ref, left, right, total):
    step = pl.program_id(0)
    planes, _, columns = field_ref.shape
    turns = HALF // 2
    row = start_ref[0] + step * 8 + lax.broadcasted_iota(jnp.int32, (8, columns), 0)
    col = lax.broadcasted_iota(jnp.int32, (8, columns), 1)
    u = (row.astype(jnp.float32) + 0.5) * (2.0 / rows_total) - 1.0
    v = (col.astype(jnp.float32) + 0.5) * (2.0 / columns) - 1.0
    inverse = lax.rsqrt(u * u + v * v)
    c1, s1 = u * inverse, v * inverse
    c2, s2 = c1 * c1 - s1 * s1, 2.0 * (c1 * s1)

    def put(ref, index, count, value):
        high, low = split(value)
        ref[pl.ds(index * 8, 8), :] = high
        ref[pl.ds((count + index) * 8, 8), :] = low

    twice = 2.0 * c2
    count = 2 * turns
    c_old, s_old = jnp.ones_like(c2), jnp.zeros_like(c2)
    c_now, s_now = c2, s2
    put(left, 0, count, c_old)
    put(left, turns, count, s_old)
    for a in range(1, turns):
        put(left, a, count, c_now)
        put(left, turns + a, count, s_now)
        c_old, s_old, c_now, s_now = c_now, s_now, twice * c_now - c_old, twice * s_now - s_old
    radial = (u, v, u * c1 - v * s1, u * s1 + v * c1)
    for z in range(planes):
        f = field_ref[z]
        for m, weight in enumerate(radial):
            put(right, z * 4 + m, 4 * planes, f * weight)
    product = lax.dot_general(
        left[...], right[...], (((1,), (1,)), ((), ())), preferred_element_type=jnp.float32
    )

    @pl.when(step == 0)
    def _():
        total[...] = product

    @pl.when(step > 0)
    def _():
        total[...] += product

    @pl.when(step == pl.num_programs(0) - 1)
    def _():
        whole = total[...]
        n = 8 * count
        m = 32 * planes
        whole = (whole[:n, :m] + whole[n:, :m]) + (whole[:n, m:] + whole[n:, m:])
        i = lax.broadcasted_iota(jnp.int32, whole.shape, 0)
        k = lax.broadcasted_iota(jnp.int32, whole.shape, 1)
        whole = jnp.where(i % 8 == k % 8, whole, 0.0)
        out_ref[...] = jnp.sum(whole.reshape(count, 8, m), axis=1)


def multipole_sums(start, field, rows_total):
    planes, rows, columns = field.shape
    turns = HALF // 2
    table = pl.pallas_call(
        functools.partial(multipole_kernel, rows_total),
        grid=(rows // 8,),
        in_specs=[smem(), pl.BlockSpec((planes, 8, columns), lambda i: (0, i, 0))],
        out_specs=pl.BlockSpec((2 * turns, 32 * planes), lambda i: (0, 0)),
        out_shape=jax.ShapeDtypeStruct((2 * turns, 32 * planes), jnp.float32),
        scratch_shapes=[
            pltpu.VMEM((32 * turns, columns), jnp.bfloat16),
            pltpu.VMEM((64 * planes, columns), jnp.bfloat16),
            pltpu.VMEM((32 * turns, 64 * planes), jnp.float32),
        ],
        compiler_params=params(),
        name="multipole",
    )(start, field)
    table = table.reshape(2, turns, planes, 2, 2, 8).sum(-1)
    cos_part = table[0, ..., 0] - table[1, ..., 1]
    sin_part = table[1, ..., 0] + table[0, ..., 1]
    order = lambda t: jnp.transpose(t, (1, 0, 2)).reshape(planes, HALF)
    return jnp.concatenate([order(cos_part), order(sin_part)], axis=1)


def swaps(pairs):
    return [(a, b) for a, b in pairs] + [(b, a) for a, b in pairs]


def reduce_rows(part):
    if lax.axis_size("gx") != 32:
        return lax.psum(part, "gx")
    even = swaps([(8 * x + z, 8 * x + z + 1) for x in range(4) for z in (0, 2, 4, 6)])
    odd = swaps([(8 * x + z, 8 * x + (z + 1) % 8) for x in range(4) for z in (1, 3, 5, 7)])
    near = swaps([(z + 8 * x, z + 8 * x + 8) for z in range(8) for x in (0, 2)])
    far = swaps([(z + 8 * x, z + (8 * x + 8) % 32) for z in range(8) for x in (1, 3)])
    swap = lambda value, pairs: lax.ppermute(value, "gx", pairs)
    pair = part + swap(part, even)
    side = swap(pair, odd)
    across = swap(side, even)
    last = swap(across, odd)
    ring = (pair + last) + (side + across)
    ring = ring + swap(ring, near)
    return ring + swap(ring, far)


def local(potential, regions, charge, levels):
    planes, row_count, columns = potential.shape
    gx, gz = lax.axis_index("gx"), lax.axis_index("gz")
    nx, nz = lax.axis_size("gx"), lax.axis_size("gz")
    rows_total = nx * row_count
    core = gz % 2
    where = jnp.stack(
        [
            core,
            gx % 2,
            jnp.where(core == 0, gz > 0, gz < nz - 1).astype(jnp.int32),
            (gx > 0).astype(jnp.int32),
            (gx < nx - 1).astype(jnp.int32),
        ]
    ).astype(jnp.int32)
    z_far = swaps([(i, (i + 1) % nz) for i in range(1, nz, 2)])
    z_near = [(i, i ^ 1) for i in range(nz)]
    x_even = [(i, i ^ 1) for i in range(nx)]
    x_odd = swaps([(i, (i + 1) % nx) for i in range(1, nx, 2)])

    def exchange(ze, zi, xe, xo):
        return (
            lax.ppermute(ze, "gz", z_far),
            lax.ppermute(zi, "gz", z_near),
            lax.ppermute(xe, "gx", x_even),
            lax.ppermute(xo, "gx", x_odd),
        )

    zero, one, charge0, charge1 = pack(potential, regions, charge, levels)
    halos = exchange(*first_send(where, one, 1))
    for sweep in range(SWEEPS):
        zero, *out = half_sweep(where, zero, one, charge0, halos, 0)
        halos = exchange(*out)
        if sweep < SWEEPS - 1:
            one, *out = half_sweep(where, one, zero, charge1, halos, 1)
            halos = exchange(*out)
        else:
            field = last_half_sweep(where, one, zero, charge1, halos)
    start = (gx * row_count).astype(jnp.int32)[None]
    part = multipole_sums(start, field, rows_total)
    part = part * (1.0 / jnp.sqrt(jnp.float32(rows_total) * jnp.float32(columns)))
    summed = reduce_rows(part)
    share = K // nx
    return field, lax.dynamic_slice_in_dim(summed, gx * share, share, 1)


def solution(mesh):
    in_specs = (P("gz", "gx", None), P("gz", "gx", None), P("gz", "gx", None), P())
    out_specs = (P("gz", "gx", None), P("gz", "gx"))
    return jax.shard_map(local, mesh=mesh, in_specs=in_specs, out_specs=out_specs, check_vma=False)
```

time: 569 us -> 136 us (0.24); the launches traced: 560 us -> 135 us
  other arithmetic: 200 us -> 0.17 us
  blocking collectives: 151 us -> 0 us
  starting transfers between devices: 100 us -> 60.6 us
  waiting for transfers between devices: 65 us -> 36.4 us
  matrix products: 27.3 us -> 0 us
  Pallas kernels: 0 us -> 24.7 us
    psum x1 -> x0, blocking collectives: 151 us -> none  [local(): summed = lax.psum(partial_terms, 'gx')]
    select_n x9 -> x0, other arithmetic: 134 us -> none  [the longest x8 116 us: relax_cells(): return jnp.where((free_cells > 0.5) & (parity_in == colour), moved, center)]
    mul x1, other arithmetic: 63.7 us -> 0.08 us  [local(): part * (1.0 / jnp.sqrt(jnp.float32(rows_total) * jnp.float32(columns)))]
    ppermute x32 -> x38, starting transfers between devices: 100 us -> 60.6 us  [the longest x8 44.4 us: exchange(): lax.ppermute(xo, 'gx', x_odd)]
    ppermute x32 -> x38, waiting for transfers between devices: 65 us -> 36.4 us  [the longest x6 22.4 us: reduce_rows(): swap = lambda value, pairs: lax.ppermute(value, 'gx', pairs)]
    dot_general x4 -> x0, matrix products: 27.3 us -> none  [local(): jnp.einsum('zxy,kxy->zk', field_now[:, start:start + block], basis_table,...]
    pallas_call x0 -> x11, Pallas kernels: none -> 24.7 us  [the longest x7 11.4 us: half_sweep(): pl.pallas_call(functools.partial(relax_kernel, colour), in_specs=[smem()]...]
    slice x9 -> x0, local copies, waits for them, and re-layouts: 9.46 us -> none  [the longest x8 7.49 us: extended(): lax.slice_in_dim(cells, cells.shape[dim] - width, cells.shape[dim], axis=...]
  transfers between devices with their start and end apart: 32 -> 38, of which waited for: 29 -> 14; matrix products, arithmetic and copies ran while one was open for 12% -> 0% of each run, Pallas kernels for 0% -> 0%
where the time goes in v1:
time: 136 us; the launch traced here: 135 us
  starting transfers between devices  60.6 us (45%)
  waiting for transfers between devices  36.4 us (27%)
  Pallas kernels  24.7 us (18%)
  local copies, waits for them, and re-layouts  12.8 us (9%)
    ppermute x8, starting transfers between devices, exchange(): lax.ppermute(xo, 'gx', x_odd)  44.4 us
    ppermute x6, waiting for transfers between devices, reduce_rows(): swap = lambda value, pairs: lax.ppermute(value, 'gx', pairs)  22.4 us
    ppermute x8, waiting for transfers between devices, exchange(): lax.ppermute(xo, 'gx', x_odd)  13.9 us
    unnamed x17, local copies, waits for them, and re-layouts  11.4 us
    pallas_call x7, Pallas kernels, half_sweep(): pl.pallas_call(functools.partial(relax_kernel, colour), in_specs=[smem()]...  11.4 us
    ppermute x8, starting transfers between devices, exchange(): lax.ppermute(zi, 'gz', z_near)  10 us
    pallas_call x1, Pallas kernels, multipole_sums(): pl.pallas_call(functools.partial(multipole_kernel, rows_total), grid=(row...  7.47 us
    pallas_call x1, Pallas kernels, last_half_sweep(): pl.pallas_call(last_kernel, in_specs=[smem()] + [vmem()] * 7, out_specs=v...  3.03 us
  transfers between devices with their start and end apart: 38, of which 14 were waited for; matrix products, arithmetic and copies ran while one was open for 0% of the time, Pallas kernels for 0%

profile of v1, /device:TPU:8, one launch (start us, length us, event | category | flops | bytes accessed | tf_op | source)
XLA Modules:
  0.0 135.5 jit_solution(15366926593694354235)
XLA Ops:
  1.3 1.6 %copy-done.1 = f32[4,64,2048]{2,1,0:T(8,128)S(1)} copy-done((f32[4,64,2048]{2,1,0:T(8,128)S(1)}, f32[4,64,2048]{2,1,0:T(8,128)}, u32[]{:S(2)}) %copy-start.1) | copy-done | bytes 2097176
  2.9 1.6 %copy-done.2 = s32[4,64,2048]{2,1,0:T(8,128)S(1)} copy-done((s32[4,64,2048]{2,1,0:T(8,128)S(1)}, s32[4,64,2048]{2,1,0:T(8,128)}, u32[]{:S(2)}) %copy-start.2) | copy-done | bytes 2097176
  4.5 1.6 %copy-done.3 = f32[4,64,2048]{2,1,0:T(8,128)S(1)} copy-done((f32[4,64,2048]{2,1,0:T(8,128)S(1)}, f32[4,64,2048]{2,1,0:T(8,128)}, u32[]{:S(2)}) %copy-start.3) | copy-done | bytes 2097176
  6.1 2.2 %pack.1 = (f32[4,32,2048]{2,1,0:T(8,128)S(1)}, f32[4,32,2048]{2,1,0:T(8,128)S(1)}, f32[4,32,2048]{2,1,0:T(8,128)S(1)}, f32[4,32,2048]{2,1,0:T(8,128)S(1)}) custom-call(f32[4,64,2048]{2,1,0:T(8,128)S(1)} %copy-done.1, s32[4,64,2048]{2,1,0:T(8,128)S(1)} %copy-done.2, f32[4,64,2048]{2,1,0:T(8,128)S(1)} %copy-done.3, f32[1,128]{1,0:T(1,128)S(1)} %pad_bitcast_fusion.lev_ref), custom_call_target="tpu_custom_call" | custom-call | tf_op jit(solution)/shard_map/pack/pallas_call | solution.py:56
  8.3 1.0 copy-done.4
  10.1 1.7 %collective-permute-start.1 = (f32[32,2048]{1,0:T(8,128)S(1)}, f32[32,2048]{1,0:T(8,128)S(1)}, u32[]{:S(2)}, u32[]{:S(2)}) collective-permute-start(f32[32,2048]{1,0:T(8,128)S(1)} %get-tuple-element.49), channel_id=1, source_target_pairs={{0,1},{1,0},{2,3},{3,2},{4,5},{5,4},{6,7},{7,6},{8,9},{9,8},{10,11... | collective-permute-start | bytes 786440 | tf_op jit(solution)/shard_map/ppermute | solution.py:335
  11.8 1.9 %collective-permute-start.2 = (f32[2,2048]{1,0:T(2,128)S(1)}, f32[2,2048]{1,0:T(2,128)S(1)}, u32[]{:S(2)}, u32[]{:S(2)}) collective-permute-start(f32[2,2048]{1,0:T(2,128)S(1)} %get-tuple-element.50), channel_id=1, source_target_pairs={{0,8},{8,0},{16,24},{24,16},{32,40},{40,32},{48,56},{56,48},{64,72... | collective-permute-start | bytes 49160 | tf_op jit(solution)/shard_map/ppermute | solution.py:336
  13.7 7.1 %collective-permute-start.3 = (f32[2,2048]{1,0:T(2,128)S(1)}, f32[2,2048]{1,0:T(2,128)S(1)}, u32[]{:S(2)}, u32[]{:S(2)}) collective-permute-start(f32[2,2048]{1,0:T(2,128)S(1)} %get-tuple-element.51), channel_id=1, source_target_pairs={{8,16},{24,32},{40,48},{56,64},{72,80},{88,96},{104,112},{120,128}... | collective-permute-start | bytes 49160 | tf_op jit(solution)/shard_map/ppermute | solution.py:337
  20.8 1.7 %collective-permute-done.3.xo_ref = f32[2,2048]{1,0:T(2,128)S(1)} collective-permute-done((f32[2,2048]{1,0:T(2,128)S(1)}, f32[2,2048]{1,0:T(2,128)S(1)}, u32[]{:S(2)}, u32[]{:S(2)}) %collective-permute-start.3) | collective-permute-done | bytes 16416 | tf_op jit(solution)/shard_map/ppermute | solution.py:337
  22.5 1.2 copy-done.5
  23.8 1.5 %relax.7 = (f32[4,32,2048]{2,1,0:T(8,128)S(1)}, f32[32,2048]{1,0:T(8,128)S(1)}, f32[32,2048]{1,0:T(8,128)S(1)}, f32[2,2048]{1,0:T(2,128)S(1)}, f32[2,2048]{1,0:T(2,128)S(1)}) custom-call(s32[5]{0:T(128)S(1)} %stack.35.where, f32[4,32,2048]{2,1,0:T(8,128)S(1)} %copy-done.5, f32[4,32,2048]{2,1,0:T(8,128)S(1)} %get-tuple-element.45.field_ref.other_ref.own_ref, ...), custom_call_target="tpu_custom_call" | custom-call | tf_op jit(solution)/shard_map/relax/pallas_call | solution.py:183
  25.5 1.2 collective-permute-start.5
  26.8 5.3 %collective-permute-start.7 = (f32[2,2048]{1,0:T(2,128)S(1)}, f32[2,2048]{1,0:T(2,128)S(1)}, u32[]{:S(2)}, u32[]{:S(2)}) collective-permute-start(f32[2,2048]{1,0:T(2,128)S(1)} %get-tuple-element.57), channel_id=1, source_target_pairs={{8,16},{24,32},{40,48},{56,64},{72,80},{88,96},{104,112},{120,128}... | collective-permute-start | bytes 49160 | tf_op jit(solution)/shard_map/ppermute | solution.py:337
  32.1 1.7 %collective-permute-done.7.xo_ref = f32[2,2048]{1,0:T(2,128)S(1)} collective-permute-done((f32[2,2048]{1,0:T(2,128)S(1)}, f32[2,2048]{1,0:T(2,128)S(1)}, u32[]{:S(2)}, u32[]{:S(2)}) %collective-permute-start.7) | collective-permute-done | bytes 16416 | tf_op jit(solution)/shard_map/ppermute | solution.py:337
  33.8 1.5 %relax.8 = (f32[4,32,2048]{2,1,0:T(8,128)S(1)}, f32[32,2048]{1,0:T(8,128)S(1)}, f32[32,2048]{1,0:T(8,128)S(1)}, f32[2,2048]{1,0:T(2,128)S(1)}, f32[2,2048]{1,0:T(2,128)S(1)}) custom-call(s32[5]{0:T(128)S(1)} %stack.35.where, f32[4,32,2048]{2,1,0:T(8,128)S(1)} %get-tuple-element.45.field_ref.other_ref.own_ref, ...), custom_call_target="tpu_custom_call" | custom-call | tf_op jit(solution)/shard_map/relax/pallas_call | solution.py:183
  35.8 5.3 %collective-permute-start.11 = (f32[2,2048]{1,0:T(2,128)S(1)}, f32[2,2048]{1,0:T(2,128)S(1)}, u32[]{:S(2)}, u32[]{:S(2)}) collective-permute-start(f32[2,2048]{1,0:T(2,128)S(1)} %get-tuple-element.62), channel_id=1, source_target_pairs={{8,16},{24,32},{40,48},{56,64},{72,80},{88,96},{104,112},{120,128}... | collective-permute-start | bytes 49160 | tf_op jit(solution)/shard_map/ppermute | solution.py:337
  41.2 1.7 %collective-permute-done.11.xo_ref = f32[2,2048]{1,0:T(2,128)S(1)} collective-permute-done((f32[2,2048]{1,0:T(2,128)S(1)}, f32[2,2048]{1,0:T(2,128)S(1)}, u32[]{:S(2)}, u32[]{:S(2)}) %collective-permute-start.11) | collective-permute-done | bytes 16416 | tf_op jit(solution)/shard_map/ppermute | solution.py:337
  42.9 1.5 %relax.9 = (f32[4,32,2048]{2,1,0:T(8,128)S(1)}, f32[32,2048]{1,0:T(8,128)S(1)}, f32[32,2048]{1,0:T(8,128)S(1)}, f32[2,2048]{1,0:T(2,128)S(1)}, f32[2,2048]{1,0:T(2,128)S(1)}) custom-call(s32[5]{0:T(128)S(1)} %stack.35.where, f32[4,32,2048]{2,1,0:T(8,128)S(1)} %get-tuple-element.52.other_ref.own_ref, f32[4,32,2048]{2,1,0:T(8,128)S(1)} %get-tuple-element.58.other_ref.own_ref, ...), custom_call_target="tpu_custom_call" | custom-call | tf_op jit(solution)/shard_map/relax/pallas_call | solution.py:183
  45.0 1.9 %collective-permute-start.13 = (f32[32,2048]{1,0:T(8,128)S(1)}, f32[32,2048]{1,0:T(8,128)S(1)}, u32[]{:S(2)}, u32[]{:S(2)}) collective-permute-start(f32[32,2048]{1,0:T(8,128)S(1)} %get-tuple-element.65), channel_id=1, source_target_pairs={{0,1},{1,0},{2,3},{3,2},{4,5},{5,4},{6,7},{7,6},{8,9},{9,8},{10,11... | collective-permute-start | bytes 786440 | tf_op jit(solution)/shard_map/ppermute | solution.py:335
  46.9 5.3 %collective-permute-start.15 = (f32[2,2048]{1,0:T(2,128)S(1)}, f32[2,2048]{1,0:T(2,128)S(1)}, u32[]{:S(2)}, u32[]{:S(2)}) collective-permute-start(f32[2,2048]{1,0:T(2,128)S(1)} %get-tuple-element.67), channel_id=1, source_target_pairs={{8,16},{24,32},{40,48},{56,64},{72,80},{88,96},{104,112},{120,128}... | collective-permute-start | bytes 49160 | tf_op jit(solution)/shard_map/ppermute | solution.py:337
  52.3 1.7 %collective-permute-done.15.xo_ref = f32[2,2048]{1,0:T(2,128)S(1)} collective-permute-done((f32[2,2048]{1,0:T(2,128)S(1)}, f32[2,2048]{1,0:T(2,128)S(1)}, u32[]{:S(2)}, u32[]{:S(2)}) %collective-permute-start.15) | collective-permute-done | bytes 16416 | tf_op jit(solution)/shard_map/ppermute | solution.py:337
  54.0 1.6 %relax.10 = (f32[4,32,2048]{2,1,0:T(8,128)S(1)}, f32[32,2048]{1,0:T(8,128)S(1)}, f32[32,2048]{1,0:T(8,128)S(1)}, f32[2,2048]{1,0:T(2,128)S(1)}, f32[2,2048]{1,0:T(2,128)S(1)}) custom-call(s32[5]{0:T(128)S(1)} %stack.35.where, f32[4,32,2048]{2,1,0:T(8,128)S(1)} %get-tuple-element.58.other_ref.own_ref, f32[4,32,2048]{2,1,0:T(8,128)S(1)} %get-tuple-element.63.other_ref.own_ref, ...), custom_call_target="tpu_custom_call" | custom-call | tf_op jit(solution)/shard_map/relax/pallas_call | solution.py:183
  55.7 0.9 collective-permute-start.17
  56.6 5.3 %collective-permute-start.19 = (f32[2,2048]{1,0:T(2,128)S(1)}, f32[2,2048]{1,0:T(2,128)S(1)}, u32[]{:S(2)}, u32[]{:S(2)}) collective-permute-start(f32[2,2048]{1,0:T(2,128)S(1)} %get-tuple-element.72), channel_id=1, source_target_pairs={{8,16},{24,32},{40,48},{56,64},{72,80},{88,96},{104,112},{120,128}... | collective-permute-start | bytes 49160 | tf_op jit(solution)/shard_map/ppermute | solution.py:337
  61.9 1.7 %collective-permute-done.19.xo_ref = f32[2,2048]{1,0:T(2,128)S(1)} collective-permute-done((f32[2,2048]{1,0:T(2,128)S(1)}, f32[2,2048]{1,0:T(2,128)S(1)}, u32[]{:S(2)}, u32[]{:S(2)}) %collective-permute-start.19) | collective-permute-done | bytes 16416 | tf_op jit(solution)/shard_map/ppermute | solution.py:337
  63.7 1.6 %relax.11 = (f32[4,32,2048]{2,1,0:T(8,128)S(1)}, f32[32,2048]{1,0:T(8,128)S(1)}, f32[32,2048]{1,0:T(8,128)S(1)}, f32[2,2048]{1,0:T(2,128)S(1)}, f32[2,2048]{1,0:T(2,128)S(1)}) custom-call(s32[5]{0:T(128)S(1)} %stack.35.where, f32[4,32,2048]{2,1,0:T(8,128)S(1)} %get-tuple-element.63.other_ref.own_ref, f32[4,32,2048]{2,1,0:T(8,128)S(1)} %get-tuple-element.68.other_ref.own_ref, ...), custom_call_target="tpu_custom_call" | custom-call | tf_op jit(solution)/shard_map/relax/pallas_call | solution.py:183
  65.3 1.4 %collective-permute-start.21 = (f32[32,2048]{1,0:T(8,128)S(1)}, f32[32,2048]{1,0:T(8,128)S(1)}, u32[]{:S(2)}, u32[]{:S(2)}) collective-permute-start(f32[32,2048]{1,0:T(8,128)S(1)} %get-tuple-element.75), channel_id=1, source_target_pairs={{0,1},{1,0},{2,3},{3,2},{4,5},{5,4},{6,7},{7,6},{8,9},{9,8},{10,11... | collective-permute-start | bytes 786440 | tf_op jit(solution)/shard_map/ppermute | solution.py:335
  66.7 5.3 %collective-permute-start.23 = (f32[2,2048]{1,0:T(2,128)S(1)}, f32[2,2048]{1,0:T(2,128)S(1)}, u32[]{:S(2)}, u32[]{:S(2)}) collective-permute-start(f32[2,2048]{1,0:T(2,128)S(1)} %get-tuple-element.77), channel_id=1, source_target_pairs={{8,16},{24,32},{40,48},{56,64},{72,80},{88,96},{104,112},{120,128}... | collective-permute-start | bytes 49160 | tf_op jit(solution)/shard_map/ppermute | solution.py:337
  72.0 1.7 %collective-permute-done.23.xo_ref = f32[2,2048]{1,0:T(2,128)S(1)} collective-permute-done((f32[2,2048]{1,0:T(2,128)S(1)}, f32[2,2048]{1,0:T(2,128)S(1)}, u32[]{:S(2)}, u32[]{:S(2)}) %collective-permute-start.23) | collective-permute-done | bytes 16416 | tf_op jit(solution)/shard_map/ppermute | solution.py:337
  73.8 1.5 %relax.12 = (f32[4,32,2048]{2,1,0:T(8,128)S(1)}, f32[32,2048]{1,0:T(8,128)S(1)}, f32[32,2048]{1,0:T(8,128)S(1)}, f32[2,2048]{1,0:T(2,128)S(1)}, f32[2,2048]{1,0:T(2,128)S(1)}) custom-call(s32[5]{0:T(128)S(1)} %stack.35.where, f32[4,32,2048]{2,1,0:T(8,128)S(1)} %get-tuple-element.68.other_ref.own_ref, f32[4,32,2048]{2,1,0:T(8,128)S(1)} %get-tuple-element.73.other_ref.own_ref, ...), custom_call_target="tpu_custom_call" | custom-call | tf_op jit(solution)/shard_map/relax/pallas_call | solution.py:183
  76.1 5.2 %collective-permute-start.27 = (f32[2,2048]{1,0:T(2,128)S(1)}, f32[2,2048]{1,0:T(2,128)S(1)}, u32[]{:S(2)}, u32[]{:S(2)}) collective-permute-start(f32[2,2048]{1,0:T(2,128)S(1)} %get-tuple-element.82), channel_id=1, source_target_pairs={{8,16},{24,32},{40,48},{56,64},{72,80},{88,96},{104,112},{120,128}... | collective-permute-start | bytes 49160 | tf_op jit(solution)/shard_map/ppermute | solution.py:337
  81.2 1.9 %collective-permute-done.27.xo_ref = f32[2,2048]{1,0:T(2,128)S(1)} collective-permute-done((f32[2,2048]{1,0:T(2,128)S(1)}, f32[2,2048]{1,0:T(2,128)S(1)}, u32[]{:S(2)}, u32[]{:S(2)}) %collective-permute-start.27) | collective-permute-done | bytes 16416 | tf_op jit(solution)/shard_map/ppermute | solution.py:337
  83.1 2.2 %relax.13 = (f32[4,32,2048]{2,1,0:T(8,128)S(1)}, f32[32,2048]{1,0:T(8,128)}, f32[32,2048]{1,0:T(8,128)S(1)}, f32[2,2048]{1,0:T(2,128)S(1)}, f32[2,2048]{1,0:T(2,128)S(1)}) custom-call(s32[5]{0:T(128)S(1)} %stack.35.where, f32[4,32,2048]{2,1,0:T(8,128)S(1)} %get-tuple-element.73.other_ref.own_ref, f32[4,32,2048]{2,1,0:T(8,128)S(1)} %get-tuple-element.78.other_ref.own_ref, ...), custom_call_target="tpu_custom_call" | custom-call | tf_op jit(solution)/shard_map/relax/pallas_call | solution.py:183
  85.3 1.0 copy-done.6
  86.5 1.9 %collective-permute-start.29 = (f32[32,2048]{1,0:T(8,128)S(1)}, f32[32,2048]{1,0:T(8,128)S(1)}, u32[]{:S(2)}, u32[]{:S(2)}) collective-permute-start(f32[32,2048]{1,0:T(8,128)S(1)} %get-tuple-element.85), channel_id=1, source_target_pairs={{0,1},{1,0},{2,3},{3,2},{4,5},{5,4},{6,7},{7,6},{8,9},{9,8},{10,11... | collective-permute-start | bytes 786440 | tf_op jit(solution)/shard_map/ppermute | solution.py:335
  88.4 5.3 %collective-permute-start.31 = (f32[2,2048]{1,0:T(2,128)S(1)}, f32[2,2048]{1,0:T(2,128)S(1)}, u32[]{:S(2)}, u32[]{:S(2)}) collective-permute-start(f32[2,2048]{1,0:T(2,128)S(1)} %get-tuple-element.87), channel_id=1, source_target_pairs={{8,16},{24,32},{40,48},{56,64},{72,80},{88,96},{104,112},{120,128}... | collective-permute-start | bytes 49160 | tf_op jit(solution)/shard_map/ppermute | solution.py:337
  93.7 1.7 %collective-permute-done.31.xo_ref = f32[2,2048]{1,0:T(2,128)S(1)} collective-permute-done((f32[2,2048]{1,0:T(2,128)S(1)}, f32[2,2048]{1,0:T(2,128)S(1)}, u32[]{:S(2)}, u32[]{:S(2)}) %collective-permute-start.31) | collective-permute-done | bytes 16416 | tf_op jit(solution)/shard_map/ppermute | solution.py:337
  95.5 1.2 copy-done.7
  96.7 3.0 %relax_last.1.field_ref = f32[4,64,2048]{2,1,0:T(8,128)} custom-call(s32[5]{0:T(128)S(1)} %stack.35.where, f32[4,32,2048]{2,1,0:T(8,128)S(1)} %get-tuple-element.78.other_ref.own_ref, f32[4,32,2048]{2,1,0:T(8,128)S(1)} %copy-done.7, f32[4,32,2048]{2,1,0:T(8,128)S(1)} %get-tuple-element.53.charge_ref, f32[32,2048]{1,0:T(8,128)S(1)} %collective-permute-done.28.ze_ref, ...), custom_call_target="tpu_custom_call" | custom-call | tf_op jit(solution)/shard_map/relax_last/pallas_call | solution.py:195
  99.7 1.6 %copy-done = f32[4,64,2048]{2,1,0:T(8,128)S(1)} copy-done((f32[4,64,2048]{2,1,0:T(8,128)S(1)}, f32[4,64,2048]{2,1,0:T(8,128)}, u32[]{:S(2)}) %copy-start) | copy-done | bytes 2097176
  101.3 7.5 %multipole.1 = f32[32,128]{1,0:T(8,128)S(1)} custom-call(s32[1]{0:T(128)} %bitcast.6.start_ref, f32[4,64,2048]{2,1,0:T(8,128)S(1)} %copy-done), custom_call_target="tpu_custom_call" | custom-call | tf_op jit(solution)/shard_map/multipole/pallas_call | solution.py:270
  109.6 3.6 %collective-permute-done.32 = f32[4,64]{1,0:T(4,128)S(1)} collective-permute-done((f32[4,64]{1,0:T(4,128)S(1)}, f32[4,64]{1,0:T(4,128)S(1)}, u32[]{:S(2)}, u32[]{:S(2)}) %collective-permute-start.32) | collective-permute-done | bytes 1056 | tf_op jit(solution)/shard_map/ppermute | solution.py:302
  113.2 4.8 %collective-permute-done.33 = f32[4,64]{1,0:T(4,128)S(1)} collective-permute-done((f32[4,64]{1,0:T(4,128)S(1)}, f32[4,64]{1,0:T(4,128)S(1)}, u32[]{:S(2)}, u32[]{:S(2)}) %collective-permute-start.33) | collective-permute-done | bytes 1056 | tf_op jit(solution)/shard_map/ppermute | solution.py:302
  118.0 3.6 %collective-permute-done.34 = f32[4,64]{1,0:T(4,128)S(1)} collective-permute-done((f32[4,64]{1,0:T(4,128)S(1)}, f32[4,64]{1,0:T(4,128)S(1)}, u32[]{:S(2)}, u32[]{:S(2)}) %collective-permute-start.34) | collective-permute-done | bytes 1056 | tf_op jit(solution)/shard_map/ppermute | solution.py:302
  121.6 4.8 %collective-permute-done.35 = f32[4,64]{1,0:T(4,128)S(1)} collective-permute-done((f32[4,64]{1,0:T(4,128)S(1)}, f32[4,64]{1,0:T(4,128)S(1)}, u32[]{:S(2)}, u32[]{:S(2)}) %collective-permute-start.35) | collective-permute-done | bytes 1056 | tf_op jit(solution)/shard_map/ppermute | solution.py:302
  126.4 3.6 %collective-permute-done.36 = f32[4,64]{1,0:T(4,128)S(1)} collective-permute-done((f32[4,64]{1,0:T(4,128)S(1)}, f32[4,64]{1,0:T(4,128)S(1)}, u32[]{:S(2)}, u32[]{:S(2)}) %collective-permute-start.36) | collective-permute-done | bytes 1056 | tf_op jit(solution)/shard_map/ppermute | solution.py:302
  130.0 2.7 %collective-permute-start.37 = (f32[4,64]{1,0:T(4,128)S(1)}, f32[4,64]{1,0:T(4,128)S(1)}, u32[]{:S(2)}, u32[]{:S(2)}) collective-permute-start(f32[4,64]{1,0:T(4,128)S(1)} %add.44), channel_id=1, source_target_pairs={{64,128},{192,0},{72,136},{200,8},{80,144},{208,16},{88,152},{216,... | collective-permute-start | bytes 3080 | tf_op jit(solution)/shard_map/ppermute | solution.py:302
  132.6 2.1 %collective-permute-done.37 = f32[4,64]{1,0:T(4,128)S(1)} collective-permute-done((f32[4,64]{1,0:T(4,128)S(1)}, f32[4,64]{1,0:T(4,128)S(1)}, u32[]{:S(2)}, u32[]{:S(2)}) %collective-permute-start.37) | collective-permute-done | bytes 1056 | tf_op jit(solution)/shard_map/ppermute | solution.py:302
  (73 shorter events, 5.5 us)
Async XLA Ops:
  1.3 1.6 %copy-start.1 = (f32[4,64,2048]{2,1,0:T(8,128)S(1)}, f32[4,64,2048]{2,1,0:T(8,128)}, u32[]{:S(2)}) copy-start(f32[4,64,2048]{2,1,0:T(8,128)} %pot_ref.1) | copy-start | bytes 6291460
  2.9 1.6 %copy-start.2 = (s32[4,64,2048]{2,1,0:T(8,128)S(1)}, s32[4,64,2048]{2,1,0:T(8,128)}, u32[]{:S(2)}) copy-start(s32[4,64,2048]{2,1,0:T(8,128)} %reg_ref.1) | copy-start | bytes 6291460
  4.5 1.6 %copy-start.3 = (f32[4,64,2048]{2,1,0:T(8,128)S(1)}, f32[4,64,2048]{2,1,0:T(8,128)}, u32[]{:S(2)}) copy-start(f32[4,64,2048]{2,1,0:T(8,128)} %chg_ref.1) | copy-start | bytes 6291460
  8.3 1.0 copy-start.4
  10.0 12.6 %collective-permute-start = (f32[32,2048]{1,0:T(8,128)S(1)}, f32[32,2048]{1,0:T(8,128)S(1)}, u32[]{:S(2)}, u32[]{:S(2)}) collective-permute-start(f32[32,2048]{1,0:T(8,128)S(1)} %get-tuple-element.48), channel_id=1, source_target_pairs={{1,2},{3,4},{5,6},{7,0},{2,1},{4,3},{6,5},{0,7},{9,10},{11,12},{13... | collective-permute-start | bytes 786440 | tf_op jit(solution)/shard_map/ppermute | solution.py:334
  10.1 12.5 %collective-permute-start.1 = (f32[32,2048]{1,0:T(8,128)S(1)}, f32[32,2048]{1,0:T(8,128)S(1)}, u32[]{:S(2)}, u32[]{:S(2)}) collective-permute-start(f32[32,2048]{1,0:T(8,128)S(1)} %get-tuple-element.49), channel_id=1, source_target_pairs={{0,1},{1,0},{2,3},{3,2},{4,5},{5,4},{6,7},{7,6},{8,9},{9,8},{10,11... | collective-permute-start | bytes 786440 | tf_op jit(solution)/shard_map/ppermute | solution.py:335
  11.8 9.1 %collective-permute-start.2 = (f32[2,2048]{1,0:T(2,128)S(1)}, f32[2,2048]{1,0:T(2,128)S(1)}, u32[]{:S(2)}, u32[]{:S(2)}) collective-permute-start(f32[2,2048]{1,0:T(2,128)S(1)} %get-tuple-element.50), channel_id=1, source_target_pairs={{0,8},{8,0},{16,24},{24,16},{32,40},{40,32},{48,56},{56,48},{64,72... | collective-permute-start | bytes 49160 | tf_op jit(solution)/shard_map/ppermute | solution.py:336
  13.7 8.9 %collective-permute-start.3 = (f32[2,2048]{1,0:T(2,128)S(1)}, f32[2,2048]{1,0:T(2,128)S(1)}, u32[]{:S(2)}, u32[]{:S(2)}) collective-permute-start(f32[2,2048]{1,0:T(2,128)S(1)} %get-tuple-element.51), channel_id=1, source_target_pairs={{8,16},{24,32},{40,48},{56,64},{72,80},{88,96},{104,112},{120,128}... | collective-permute-start | bytes 49160 | tf_op jit(solution)/shard_map/ppermute | solution.py:337
  22.5 1.2 copy-start.5
  25.3 8.6 %collective-permute-start.4 = (f32[32,2048]{1,0:T(8,128)S(1)}, f32[32,2048]{1,0:T(8,128)S(1)}, u32[]{:S(2)}, u32[]{:S(2)}) collective-permute-start(f32[32,2048]{1,0:T(8,128)S(1)} %get-tuple-element.54), channel_id=1, source_target_pairs={{1,2},{3,4},{5,6},{7,0},{2,1},{4,3},{6,5},{0,7},{9,10},{11,12},{13... | collective-permute-start | bytes 786440 | tf_op jit(solution)/shard_map/ppermute | solution.py:334
  25.5 8.3 %collective-permute-start.5 = (f32[32,2048]{1,0:T(8,128)S(1)}, f32[32,2048]{1,0:T(8,128)S(1)}, u32[]{:S(2)}, u32[]{:S(2)}) collective-permute-start(f32[32,2048]{1,0:T(8,128)S(1)} %get-tuple-element.55), channel_id=1, source_target_pairs={{0,1},{1,0},{2,3},{3,2},{4,5},{5,4},{6,7},{7,6},{8,9},{9,8},{10,11... | collective-permute-start | bytes 786440 | tf_op jit(solution)/shard_map/ppermute | solution.py:335
  26.8 5.3 %collective-permute-start.6 = (f32[2,2048]{1,0:T(2,128)S(1)}, f32[2,2048]{1,0:T(2,128)S(1)}, u32[]{:S(2)}, u32[]{:S(2)}) collective-permute-start(f32[2,2048]{1,0:T(2,128)S(1)} %get-tuple-element.56), channel_id=1, source_target_pairs={{0,8},{8,0},{16,24},{24,16},{32,40},{40,32},{48,56},{56,48},{64,72... | collective-permute-start | bytes 49160 | tf_op jit(solution)/shard_map/ppermute | solution.py:336
  26.8 7.1 %collective-permute-start.7 = (f32[2,2048]{1,0:T(2,128)S(1)}, f32[2,2048]{1,0:T(2,128)S(1)}, u32[]{:S(2)}, u32[]{:S(2)}) collective-permute-start(f32[2,2048]{1,0:T(2,128)S(1)} %get-tuple-element.57), channel_id=1, source_target_pairs={{8,16},{24,32},{40,48},{56,64},{72,80},{88,96},{104,112},{120,128}... | collective-permute-start | bytes 49160 | tf_op jit(solution)/shard_map/ppermute | solution.py:337
  35.4 7.5 %collective-permute-start.8 = (f32[32,2048]{1,0:T(8,128)S(1)}, f32[32,2048]{1,0:T(8,128)S(1)}, u32[]{:S(2)}, u32[]{:S(2)}) collective-permute-start(f32[32,2048]{1,0:T(8,128)S(1)} %get-tuple-element.59), channel_id=1, source_target_pairs={{1,2},{3,4},{5,6},{7,0},{2,1},{4,3},{6,5},{0,7},{9,10},{11,12},{13... | collective-permute-start | bytes 786440 | tf_op jit(solution)/shard_map/ppermute | solution.py:334
  35.5 7.4 %collective-permute-start.9 = (f32[32,2048]{1,0:T(8,128)S(1)}, f32[32,2048]{1,0:T(8,128)S(1)}, u32[]{:S(2)}, u32[]{:S(2)}) collective-permute-start(f32[32,2048]{1,0:T(8,128)S(1)} %get-tuple-element.60), channel_id=1, source_target_pairs={{0,1},{1,0},{2,3},{3,2},{4,5},{5,4},{6,7},{7,6},{8,9},{9,8},{10,11... | collective-permute-start | bytes 786440 | tf_op jit(solution)/shard_map/ppermute | solution.py:335
  35.8 5.3 %collective-permute-start.10 = (f32[2,2048]{1,0:T(2,128)S(1)}, f32[2,2048]{1,0:T(2,128)S(1)}, u32[]{:S(2)}, u32[]{:S(2)}) collective-permute-start(f32[2,2048]{1,0:T(2,128)S(1)} %get-tuple-element.61), channel_id=1, source_target_pairs={{0,8},{8,0},{16,24},{24,16},{32,40},{40,32},{48,56},{56,48},{64,72... | collective-permute-start | bytes 49160 | tf_op jit(solution)/shard_map/ppermute | solution.py:336
  35.8 7.1 %collective-permute-start.11 = (f32[2,2048]{1,0:T(2,128)S(1)}, f32[2,2048]{1,0:T(2,128)S(1)}, u32[]{:S(2)}, u32[]{:S(2)}) collective-permute-start(f32[2,2048]{1,0:T(2,128)S(1)} %get-tuple-element.62), channel_id=1, source_target_pairs={{8,16},{24,32},{40,48},{56,64},{72,80},{88,96},{104,112},{120,128}... | collective-permute-start | bytes 49160 | tf_op jit(solution)/shard_map/ppermute | solution.py:337
  44.4 9.6 %collective-permute-start.12 = (f32[32,2048]{1,0:T(8,128)S(1)}, f32[32,2048]{1,0:T(8,128)S(1)}, u32[]{:S(2)}, u32[]{:S(2)}) collective-permute-start(f32[32,2048]{1,0:T(8,128)S(1)} %get-tuple-element.64), channel_id=1, source_target_pairs={{1,2},{3,4},{5,6},{7,0},{2,1},{4,3},{6,5},{0,7},{9,10},{11,12},{13... | collective-permute-start | bytes 786440 | tf_op jit(solution)/shard_map/ppermute | solution.py:334
  45.0 9.0 %collective-permute-start.13 = (f32[32,2048]{1,0:T(8,128)S(1)}, f32[32,2048]{1,0:T(8,128)S(1)}, u32[]{:S(2)}, u32[]{:S(2)}) collective-permute-start(f32[32,2048]{1,0:T(8,128)S(1)} %get-tuple-element.65), channel_id=1, source_target_pairs={{0,1},{1,0},{2,3},{3,2},{4,5},{5,4},{6,7},{7,6},{8,9},{9,8},{10,11... | collective-permute-start | bytes 786440 | tf_op jit(solution)/shard_map/ppermute | solution.py:335
  46.9 5.3 %collective-permute-start.14 = (f32[2,2048]{1,0:T(2,128)S(1)}, f32[2,2048]{1,0:T(2,128)S(1)}, u32[]{:S(2)}, u32[]{:S(2)}) collective-permute-start(f32[2,2048]{1,0:T(2,128)S(1)} %get-tuple-element.66), channel_id=1, source_target_pairs={{0,8},{8,0},{16,24},{24,16},{32,40},{40,32},{48,56},{56,48},{64,72... | collective-permute-start | bytes 49160 | tf_op jit(solution)/shard_map/ppermute | solution.py:336
  46.9 7.1 %collective-permute-start.15 = (f32[2,2048]{1,0:T(2,128)S(1)}, f32[2,2048]{1,0:T(2,128)S(1)}, u32[]{:S(2)}, u32[]{:S(2)}) collective-permute-start(f32[2,2048]{1,0:T(2,128)S(1)} %get-tuple-element.67), channel_id=1, source_target_pairs={{8,16},{24,32},{40,48},{56,64},{72,80},{88,96},{104,112},{120,128}... | collective-permute-start | bytes 49160 | tf_op jit(solution)/shard_map/ppermute | solution.py:337
  55.6 8.1 %collective-permute-start.16 = (f32[32,2048]{1,0:T(8,128)S(1)}, f32[32,2048]{1,0:T(8,128)S(1)}, u32[]{:S(2)}, u32[]{:S(2)}) collective-permute-start(f32[32,2048]{1,0:T(8,128)S(1)} %get-tuple-element.69), channel_id=1, source_target_pairs={{1,2},{3,4},{5,6},{7,0},{2,1},{4,3},{6,5},{0,7},{9,10},{11,12},{13... | collective-permute-start | bytes 786440 | tf_op jit(solution)/shard_map/ppermute | solution.py:334
  55.7 8.0 %collective-permute-start.17 = (f32[32,2048]{1,0:T(8,128)S(1)}, f32[32,2048]{1,0:T(8,128)S(1)}, u32[]{:S(2)}, u32[]{:S(2)}) collective-permute-start(f32[32,2048]{1,0:T(8,128)S(1)} %get-tuple-element.70), channel_id=1, source_target_pairs={{0,1},{1,0},{2,3},{3,2},{4,5},{5,4},{6,7},{7,6},{8,9},{9,8},{10,11... | collective-permute-start | bytes 786440 | tf_op jit(solution)/shard_map/ppermute | solution.py:335
  56.6 5.3 %collective-permute-start.18 = (f32[2,2048]{1,0:T(2,128)S(1)}, f32[2,2048]{1,0:T(2,128)S(1)}, u32[]{:S(2)}, u32[]{:S(2)}) collective-permute-start(f32[2,2048]{1,0:T(2,128)S(1)} %get-tuple-element.71), channel_id=1, source_target_pairs={{0,8},{8,0},{16,24},{24,16},{32,40},{40,32},{48,56},{56,48},{64,72... | collective-permute-start | bytes 49160 | tf_op jit(solution)/shard_map/ppermute | solution.py:336
  56.6 7.1 %collective-permute-start.19 = (f32[2,2048]{1,0:T(2,128)S(1)}, f32[2,2048]{1,0:T(2,128)S(1)}, u32[]{:S(2)}, u32[]{:S(2)}) collective-permute-start(f32[2,2048]{1,0:T(2,128)S(1)} %get-tuple-element.72), channel_id=1, source_target_pairs={{8,16},{24,32},{40,48},{56,64},{72,80},{88,96},{104,112},{120,128}... | collective-permute-start | bytes 49160 | tf_op jit(solution)/shard_map/ppermute | solution.py:337
  65.2 8.5 %collective-permute-start.20 = (f32[32,2048]{1,0:T(8,128)S(1)}, f32[32,2048]{1,0:T(8,128)S(1)}, u32[]{:S(2)}, u32[]{:S(2)}) collective-permute-start(f32[32,2048]{1,0:T(8,128)S(1)} %get-tuple-element.74), channel_id=1, source_target_pairs={{1,2},{3,4},{5,6},{7,0},{2,1},{4,3},{6,5},{0,7},{9,10},{11,12},{13... | collective-permute-start | bytes 786440 | tf_op jit(solution)/shard_map/ppermute | solution.py:334
  65.3 8.4 %collective-permute-start.21 = (f32[32,2048]{1,0:T(8,128)S(1)}, f32[32,2048]{1,0:T(8,128)S(1)}, u32[]{:S(2)}, u32[]{:S(2)}) collective-permute-start(f32[32,2048]{1,0:T(8,128)S(1)} %get-tuple-element.75), channel_id=1, source_target_pairs={{0,1},{1,0},{2,3},{3,2},{4,5},{5,4},{6,7},{7,6},{8,9},{9,8},{10,11... | collective-permute-start | bytes 786440 | tf_op jit(solution)/shard_map/ppermute | solution.py:335
  66.7 5.3 %collective-permute-start.22 = (f32[2,2048]{1,0:T(2,128)S(1)}, f32[2,2048]{1,0:T(2,128)S(1)}, u32[]{:S(2)}, u32[]{:S(2)}) collective-permute-start(f32[2,2048]{1,0:T(2,128)S(1)} %get-tuple-element.76), channel_id=1, source_target_pairs={{0,8},{8,0},{16,24},{24,16},{32,40},{40,32},{48,56},{56,48},{64,72... | collective-permute-start | bytes 49160 | tf_op jit(solution)/shard_map/ppermute | solution.py:336
  66.7 7.1 %collective-permute-start.23 = (f32[2,2048]{1,0:T(2,128)S(1)}, f32[2,2048]{1,0:T(2,128)S(1)}, u32[]{:S(2)}, u32[]{:S(2)}) collective-permute-start(f32[2,2048]{1,0:T(2,128)S(1)} %get-tuple-element.77), channel_id=1, source_target_pairs={{8,16},{24,32},{40,48},{56,64},{72,80},{88,96},{104,112},{120,128}... | collective-permute-start | bytes 49160 | tf_op jit(solution)/shard_map/ppermute | solution.py:337
  75.3 7.8 %collective-permute-start.24 = (f32[32,2048]{1,0:T(8,128)S(1)}, f32[32,2048]{1,0:T(8,128)S(1)}, u32[]{:S(2)}, u32[]{:S(2)}) collective-permute-start(f32[32,2048]{1,0:T(8,128)S(1)} %get-tuple-element.79), channel_id=1, source_target_pairs={{1,2},{3,4},{5,6},{7,0},{2,1},{4,3},{6,5},{0,7},{9,10},{11,12},{13... | collective-permute-start | bytes 786440 | tf_op jit(solution)/shard_map/ppermute | solution.py:334
  75.4 7.7 %collective-permute-start.25 = (f32[32,2048]{1,0:T(8,128)S(1)}, f32[32,2048]{1,0:T(8,128)S(1)}, u32[]{:S(2)}, u32[]{:S(2)}) collective-permute-start(f32[32,2048]{1,0:T(8,128)S(1)} %get-tuple-element.80), channel_id=1, source_target_pairs={{0,1},{1,0},{2,3},{3,2},{4,5},{5,4},{6,7},{7,6},{8,9},{9,8},{10,11... | collective-permute-start | bytes 786440 | tf_op jit(solution)/shard_map/ppermute | solution.py:335
  76.1 5.2 %collective-permute-start.26 = (f32[2,2048]{1,0:T(2,128)S(1)}, f32[2,2048]{1,0:T(2,128)S(1)}, u32[]{:S(2)}, u32[]{:S(2)}) collective-permute-start(f32[2,2048]{1,0:T(2,128)S(1)} %get-tuple-element.81), channel_id=1, source_target_pairs={{0,8},{8,0},{16,24},{24,16},{32,40},{40,32},{48,56},{56,48},{64,72... | collective-permute-start | bytes 49160 | tf_op jit(solution)/shard_map/ppermute | solution.py:336
  76.1 7.1 %collective-permute-start.27 = (f32[2,2048]{1,0:T(2,128)S(1)}, f32[2,2048]{1,0:T(2,128)S(1)}, u32[]{:S(2)}, u32[]{:S(2)}) collective-permute-start(f32[2,2048]{1,0:T(2,128)S(1)} %get-tuple-element.82), channel_id=1, source_target_pairs={{8,16},{24,32},{40,48},{56,64},{72,80},{88,96},{104,112},{120,128}... | collective-permute-start | bytes 49160 | tf_op jit(solution)/shard_map/ppermute | solution.py:337
  85.3 1.0 copy-start.6
  86.3 9.2 %collective-permute-start.28 = (f32[32,2048]{1,0:T(8,128)}, f32[32,2048]{1,0:T(8,128)S(1)}, u32[]{:S(2)}, u32[]{:S(2)}) collective-permute-start(f32[32,2048]{1,0:T(8,128)} %get-tuple-element.84), channel_id=1, source_target_pairs={{1,2},{3,4},{5,6},{7,0},{2,1},{4,3},{6,5},{0,7},{9,10},{11,12},{13... | collective-permute-start | bytes 786440 | tf_op jit(solution)/shard_map/ppermute | solution.py:334
  86.5 9.0 %collective-permute-start.29 = (f32[32,2048]{1,0:T(8,128)S(1)}, f32[32,2048]{1,0:T(8,128)S(1)}, u32[]{:S(2)}, u32[]{:S(2)}) collective-permute-start(f32[32,2048]{1,0:T(8,128)S(1)} %get-tuple-element.85), channel_id=1, source_target_pairs={{0,1},{1,0},{2,3},{3,2},{4,5},{5,4},{6,7},{7,6},{8,9},{9,8},{10,11... | collective-permute-start | bytes 786440 | tf_op jit(solution)/shard_map/ppermute | solution.py:335
  88.4 5.3 %collective-permute-start.30 = (f32[2,2048]{1,0:T(2,128)S(1)}, f32[2,2048]{1,0:T(2,128)S(1)}, u32[]{:S(2)}, u32[]{:S(2)}) collective-permute-start(f32[2,2048]{1,0:T(2,128)S(1)} %get-tuple-element.86), channel_id=1, source_target_pairs={{0,8},{8,0},{16,24},{24,16},{32,40},{40,32},{48,56},{56,48},{64,72... | collective-permute-start | bytes 49160 | tf_op jit(solution)/shard_map/ppermute | solution.py:336
  88.4 7.1 %collective-permute-start.31 = (f32[2,2048]{1,0:T(2,128)S(1)}, f32[2,2048]{1,0:T(2,128)S(1)}, u32[]{:S(2)}, u32[]{:S(2)}) collective-permute-start(f32[2,2048]{1,0:T(2,128)S(1)} %get-tuple-element.87), channel_id=1, source_target_pairs={{8,16},{24,32},{40,48},{56,64},{72,80},{88,96},{104,112},{120,128}... | collective-permute-start | bytes 49160 | tf_op jit(solution)/shard_map/ppermute | solution.py:337
  95.5 1.2 copy-start.7
  99.7 1.6 %copy-start = (f32[4,64,2048]{2,1,0:T(8,128)S(1)}, f32[4,64,2048]{2,1,0:T(8,128)}, u32[]{:S(2)}) copy-start(f32[4,64,2048]{2,1,0:T(8,128)} %relax_last.1.field_ref) | copy-start | bytes 6291460
  109.6 3.6 %collective-permute-start.32 = (f32[4,64]{1,0:T(4,128)S(1)}, f32[4,64]{1,0:T(4,128)S(1)}, u32[]{:S(2)}, u32[]{:S(2)}) collective-permute-start(f32[4,64]{1,0:T(4,128)S(1)} %maximum_multiply_fusion), channel_id=1, source_target_pairs={{0,8},{16,24},{32,40},{48,56},{64,72},{80,88},{96,104},{112,120},{... | collective-permute-start | bytes 3080 | tf_op jit(solution)/shard_map/ppermute | solution.py:302
  113.2 4.8 %collective-permute-start.33 = (f32[4,64]{1,0:T(4,128)S(1)}, f32[4,64]{1,0:T(4,128)S(1)}, u32[]{:S(2)}, u32[]{:S(2)}) collective-permute-start(f32[4,64]{1,0:T(4,128)S(1)} %add.40), channel_id=1, source_target_pairs={{8,16},{24,32},{40,48},{56,0},{72,80},{88,96},{104,112},{120,64},{... | collective-permute-start | bytes 3080 | tf_op jit(solution)/shard_map/ppermute | solution.py:302
  118.0 3.6 %collective-permute-start.34 = (f32[4,64]{1,0:T(4,128)S(1)}, f32[4,64]{1,0:T(4,128)S(1)}, u32[]{:S(2)}, u32[]{:S(2)}) collective-permute-start(f32[4,64]{1,0:T(4,128)S(1)} %collective-permute-done.33), channel_id=1, source_target_pairs={{0,8},{16,24},{32,40},{48,56},{64,72},{80,88},{96,104},{112,120},{... | collective-permute-start | bytes 3080 | tf_op jit(solution)/shard_map/ppermute | solution.py:302
  121.6 4.8 %collective-permute-start.35 = (f32[4,64]{1,0:T(4,128)S(1)}, f32[4,64]{1,0:T(4,128)S(1)}, u32[]{:S(2)}, u32[]{:S(2)}) collective-permute-start(f32[4,64]{1,0:T(4,128)S(1)} %collective-permute-done.34), channel_id=1, source_target_pairs={{8,16},{24,32},{40,48},{56,0},{72,80},{88,96},{104,112},{120,64},{... | collective-permute-start | bytes 3080 | tf_op jit(solution)/shard_map/ppermute | solution.py:302
  126.4 3.6 %collective-permute-start.36 = (f32[4,64]{1,0:T(4,128)S(1)}, f32[4,64]{1,0:T(4,128)S(1)}, u32[]{:S(2)}, u32[]{:S(2)}) collective-permute-start(f32[4,64]{1,0:T(4,128)S(1)} %add_add_fusion), channel_id=1, source_target_pairs={{0,64},{128,192},{8,72},{136,200},{16,80},{144,208},{24,88},{152,2... | collective-permute-start | bytes 3080 | tf_op jit(solution)/shard_map/ppermute | solution.py:302
  130.0 4.8 %collective-permute-start.37 = (f32[4,64]{1,0:T(4,128)S(1)}, f32[4,64]{1,0:T(4,128)S(1)}, u32[]{:S(2)}, u32[]{:S(2)}) collective-permute-start(f32[4,64]{1,0:T(4,128)S(1)} %add.44), channel_id=1, source_target_pairs={{64,128},{192,0},{72,136},{200,8},{80,144},{208,16},{88,152},{216,... | collective-permute-start | bytes 3080 | tf_op jit(solution)/shard_map/ppermute | solution.py:302

commit v2 on v0

v2 whole, which is shorter than its diff:
```python
import functools

import jax
import jax.numpy as jnp
from jax import lax
from jax.experimental import pallas as pl
from jax.experimental.pallas import tpu as pltpu
from jax.sharding import PartitionSpec as P

K = 64
SWEEPS = 4
HALF = K // 2
TURNS = 8
STEPS = 4
LANES = 128
PINNED = 1e30
VMEM_BYTES = 16 * 1024 * 1024


def vmem():
    return pl.BlockSpec(memory_space=pltpu.VMEM)


def smem():
    return pl.BlockSpec(memory_space=pltpu.SMEM)


def hbm():
    return pl.BlockSpec(memory_space=pltpu.HBM)


def anywhere():
    return pl.BlockSpec(memory_space=pl.ANY)


def params():
    return pltpu.CompilerParams(vmem_limit_bytes=VMEM_BYTES)


def cost(flops, nbytes):
    return pl.CostEstimate(flops=flops, bytes_accessed=nbytes, transcendentals=0)


def shape_of(*shape):
    return jax.ShapeDtypeStruct(shape, jnp.float32)


def column_parity(rows, columns):
    return lax.broadcasted_iota(jnp.int32, (rows, columns), 1) % 2


def merge_rows(rows, keep):
    mask = column_parity(1, rows[0].shape[1]) == keep
    return jnp.concatenate([jnp.where(mask, rows[z], rows[z + 1]) for z in range(0, len(rows), 2)], axis=0)


def sends(ref, colour, core, odd, ze_ref, zi_ref, xe_ref, xo_ref):
    planes, rows, _ = ref.shape
    for j in range(0, rows, 8):
        at = pl.ds(j, 8)
        low, high = ref[0, at, :], ref[planes - 1, at, :]
        ze_ref[at, :] = jnp.where(core == 0, low, high)
        zi_ref[at, :] = jnp.where(core == 0, high, low)
    above = merge_rows([ref[z, pl.ds(rows - 1, 1), :] for z in range(planes)], 1 - colour)
    below = merge_rows([ref[z, pl.ds(0, 1), :] for z in range(planes)], colour)
    xe_ref[...] = jnp.where(odd == 0, above, below)
    xo_ref[...] = jnp.where(odd == 0, below, above)


def pack_kernel(where, pot_hbm, reg_hbm, chg_hbm, lev_ref, f0_ref, f1_ref, c0_ref, c1_ref, ze_ref, zi_ref, xe_ref,
                xo_ref, pot_ref, reg_ref, chg_ref, field, charge, sems):
    planes, rows, columns = f0_ref.shape
    tiles = rows // 8
    table = jnp.broadcast_to(lev_ref[...], (8, LANES))
    copies = [
        [
            pltpu.make_async_copy(source.at[z], target.at[z], sems.at[z, i])
            for i, (source, target) in enumerate(((reg_hbm, reg_ref), (pot_hbm, pot_ref), (chg_hbm, chg_ref)))
        ]
        for z in range(planes)
    ]
    for plane in copies:
        for copy in plane:
            copy.start()
    for z in range(planes):
        even = column_parity(8, LANES) == z % 2
        for copy in copies[z]:
            copy.wait()
        for c in range(columns // LANES):
            at = pl.ds(LANES * c, LANES)
            slot = z % 2 * (columns // LANES) + c
            for j in range(0, 2 * rows, 8):
                to = pl.ds(j, 8)
                region = reg_ref[z, to, at]
                pinned = jnp.take_along_axis(table, region, axis=1)
                free = region == 0
                field[slot, to, :] = jnp.where(free, pot_ref[z, to, at], pinned)
                charge[slot, to, :] = jnp.where(free, chg_ref[z, to, at], PINNED)
            for source, out0, out1 in ((field, f0_ref, f1_ref), (charge, c0_ref, c1_ref)):
                for j in range(tiles):
                    a = source[slot, pl.ds(2 * j, 8, stride=2 * tiles), :]
                    b = source[slot, pl.ds(2 * j + 1, 8, stride=2 * tiles), :]
                    out0[z, pl.ds(8 * j, 8), at] = jnp.where(even, a, b)
                    out1[z, pl.ds(8 * j, 8), at] = jnp.where(even, b, a)
    sends(f1_ref, 1, where[0], where[1], ze_ref, zi_ref, xe_ref, xo_ref)


def send_shapes(planes, rows, columns):
    return [shape_of(rows, columns)] * 2 + [shape_of(planes // 2, columns)] * 2


def pack(where, potential, regions, charge, levels):
    planes, rows, columns = potential.shape
    table = jnp.pad(levels, (0, LANES - levels.shape[0]))[None, :]
    half = shape_of(planes, rows // 2, columns)
    whole = (planes, rows, columns)
    stage = pltpu.VMEM((2 * columns // LANES, rows, LANES), jnp.float32)
    return pl.pallas_call(
        pack_kernel,
        in_specs=[smem(), hbm(), hbm(), hbm(), vmem()],
        out_specs=[vmem()] * 8,
        out_shape=[half] * 4 + send_shapes(*half.shape),
        scratch_shapes=[
            pltpu.VMEM(whole, jnp.float32),
            pltpu.VMEM(whole, jnp.int32),
            pltpu.VMEM(whole, jnp.float32),
            stage,
            stage,
            pltpu.SemaphoreType.DMA((planes, 3)),
        ],
        compiler_params=params(),
        name="pack",
    )(where, potential, regions, charge, table)


def relax(where, own_ref, other_ref, charge_ref, ze_ref, zi_ref, xe_ref, xo_ref, colour, put):
    core, odd, far_live, below_live, above_live = (where[i] for i in range(5))
    planes, rows, columns = own_ref.shape
    tiles = rows // 8
    row = lax.broadcasted_iota(jnp.int32, (8, columns), 0)
    lane = lax.broadcasted_iota(jnp.int32, (8, LANES), 1)
    parity = column_parity(8, columns)
    xe, xo = xe_ref[...], xo_ref[...]
    below = jnp.where(below_live == 1, jnp.where(odd == 0, xo, xe), 0.0)
    above = jnp.where(above_live == 1, jnp.where(odd == 0, xe, xo), 0.0)

    for z in range(planes):
        first_row = parity == (z + colour) % 2
        for j in range(tiles):
            at = pl.ds(8 * j, 8)
            tile = lambda t: other_ref[z, pl.ds(8 * t, 8), :]
            mid = tile(j)
            if z in (0, planes - 1):
                far = jnp.where(far_live == 1, ze_ref[at, :], 0.0)
                near = zi_ref[at, :]
            z_low = other_ref[z - 1, at, :] if z else jnp.where(core == 0, far, near)
            z_high = other_ref[z + 1, at, :] if z < planes - 1 else jnp.where(core == 0, near, far)
            if j:
                x_low = tile(j - 1)
            else:
                x_low = jnp.where(row == 0, below[z // 2 : z // 2 + 1], pltpu.roll(tile(tiles - 1), 1, 0))
            if j < tiles - 1:
                x_high = tile(j + 1)
            else:
                x_high = jnp.where(row == 7, above[z // 2 : z // 2 + 1], pltpu.roll(tile(0), 7, 0))
            y_low, y_high = pltpu.roll(mid, 1, 1), pltpu.roll(mid, columns - 1, 1)
            y_low = jnp.concatenate([jnp.where(lane == 0, 0.0, y_low[:, :LANES]), y_low[:, LANES:]], axis=1)
            y_high = jnp.concatenate(
                [y_high[:, :-LANES], jnp.where(lane == LANES - 1, 0.0, y_high[:, -LANES:])], axis=1
            )
            charge = charge_ref[z, at, :]
            beside = z_low + z_high + mid + jnp.where(first_row, x_low, x_high) + y_low + y_high
            own = own_ref[z, at, :]
            put(z, j, jnp.where(charge < PINNED, 0.25 * (beside + charge) - 0.5 * own, own))


def relax_kernel(colour, where, own_ref, other_ref, charge_ref, ze_ref, zi_ref, xe_ref, xo_ref, after,
                 out_ref, ze_out, zi_out, xe_out, xo_out):
    del after

    def put(z, j, value):
        out_ref[z, pl.ds(8 * j, 8), :] = value

    relax(where, own_ref, other_ref, charge_ref, ze_ref, zi_ref, xe_ref, xo_ref, colour, put)
    sends(out_ref, colour, where[0], where[1], ze_out, zi_out, xe_out, xo_out)


def half_sweep(where, own, other, charge, halos, colour, after):
    return pl.pallas_call(
        functools.partial(relax_kernel, colour),
        in_specs=[smem()] + [vmem()] * 7 + [anywhere()],
        out_specs=[vmem()] * 5,
        out_shape=[shape_of(*own.shape)] + send_shapes(*own.shape),
        compiler_params=params(),
        cost_estimate=cost(14 * own.size, 0),
        name="relax",
    )(where, own, other, charge, *halos, after)


def split(value):
    high = value.astype(jnp.bfloat16)
    return high, (value - high.astype(jnp.float32)).astype(jnp.bfloat16)


def angles_kernel(rows_total, tiles, columns, offset, start, after, left_ref, radial_ref, done_ref):
    del after
    done_ref[...] = jnp.zeros_like(done_ref)
    shape = (8, columns)
    column = lax.broadcasted_iota(jnp.int32, shape, 1)
    v = (column.astype(jnp.float32) + 0.5) * (2.0 / columns) - 1.0
    for j in range(tiles):
        packed = lax.broadcasted_iota(jnp.int32, shape, 0) * tiles + j
        row = start[0] + 2 * packed + (column + offset) % 2
        u = (row.astype(jnp.float32) + 0.5) * (2.0 / rows_total) - 1.0
        inverse = lax.rsqrt(u * u + v * v)
        c1, s1 = u * inverse, v * inverse
        c2, s2 = c1 * c1 - s1 * s1, 2.0 * (c1 * s1)
        c4, s4 = c2 * c2 - s2 * s2, 2.0 * (c2 * s2)
        u2, v2 = u * c1 - v * s1, u * s1 + v * c1
        u3, v3 = u2 * c1 - v2 * s1, u2 * s1 + v2 * c1
        u4, v4 = u2 * c2 - v2 * s2, u2 * s2 + v2 * c2
        for m, value in enumerate((u, u2, u3, u4, v, v2, v3, v4)):
            radial_ref[j, pl.ds(8 * m, 8), :] = value

        def put(index, value):
            high, low = split(value)
            left_ref[j, pl.ds(8 * index, 8), :] = high
            left_ref[j, pl.ds(8 * (2 * TURNS + index), 8), :] = low

        twice = 2.0 * c4
        c_old, s_old, c_now, s_now = jnp.ones_like(c4), jnp.zeros_like(c4), c4, s4
        put(0, c_old)
        put(TURNS, s_old)
        for a in range(1, TURNS):
            put(a, c_now)
            put(TURNS + a, s_now)
            c_old, s_old, c_now, s_now = c_now, s_now, twice * c_now - c_old, twice * s_now - s_old


def angles(start, after, rows_total, tiles, columns, offset):
    left = jax.ShapeDtypeStruct((tiles, 32 * TURNS, columns), jnp.bfloat16)
    return pl.pallas_call(
        functools.partial(angles_kernel, rows_total, tiles, columns, offset),
        in_specs=[smem(), anywhere()],
        out_specs=[vmem()] * 3,
        out_shape=[left, shape_of(tiles, 16 * STEPS, columns), shape_of(8, LANES)],
        compiler_params=params(),
        cost_estimate=cost(128 * tiles * 8 * columns, 0),
        name="angles",
    )(start, after)


def multipoles_of(colour, field_of, tables, out_ref, right):
    planes = out_ref.shape[0]
    pairs = planes // 2
    n, m = 16 * TURNS, 16 * STEPS * pairs
    tiles = tables[0][0].shape[0]
    for e in (0, 1):
        left_ref, radial_ref = tables[e]
        total = None
        for j in range(tiles):
            slot = (e * tiles + j) % right.shape[0]
            for k in range(pairs):
                f = field_of(2 * k + (e + colour) % 2, j)
                for b in range(2 * STEPS):
                    high, low = split(f * radial_ref[j, pl.ds(8 * b, 8), :])
                    index = 2 * STEPS * k + b
                    right[slot, pl.ds(8 * index, 8), :] = high
                    right[slot, pl.ds(m + 8 * index, 8), :] = low
            product = lax.dot_general(
                left_ref[j], right[slot], (((1,), (1,)), ((), ())), preferred_element_type=jnp.float32
            )
            total = product if total is None else total + product
        total = (total[:n, :m] + total[n:, :m]) + (total[:n, m:] + total[n:, m:])
        i = lax.broadcasted_iota(jnp.int32, total.shape, 0)
        k = lax.broadcasted_iota(jnp.int32, total.shape, 1)
        total = jnp.sum(jnp.where(i % 8 == k % 8, total, 0.0).reshape(2 * TURNS, 8, m), axis=1)
        for k in range(pairs):
            out_ref[2 * k + (e + colour) % 2] = total[:, 16 * STEPS * k : 16 * STEPS * (k + 1)]


def right_scratch(planes, columns):
    return pltpu.VMEM((2, 16 * STEPS * planes, columns), jnp.bfloat16)


def sums_shape(planes):
    return shape_of(planes, 2 * TURNS, 16 * STEPS)


def multipole_kernel(field_ref, left0, radial0, left1, radial1, out_ref, done_ref, right):
    done_ref[...] = jnp.zeros_like(done_ref)
    multipoles_of(0, lambda z, j: field_ref[z, pl.ds(8 * j, 8), :], ((left0, radial0), (left1, radial1)), out_ref,
                  right)


def multipole_sums(field, tables):
    planes, _, columns = field.shape
    return pl.pallas_call(
        multipole_kernel,
        in_specs=[vmem()] * 5,
        out_specs=[vmem()] * 2,
        out_shape=[sums_shape(planes), shape_of(8, LANES)],
        scratch_shapes=[right_scratch(planes, columns)],
        compiler_params=params(),
        cost_estimate=cost(100 * field.size, 0),
        name="multipole",
    )(field, *tables)


def last_kernel(where, own_ref, other_ref, charge_ref, ze_ref, zi_ref, xe_ref, xo_ref, left0, radial0, left1, radial1,
                after, field_hbm, out_ref, one, staged, right, sems):
    del after
    planes, rows, columns = own_ref.shape
    tiles = rows // 8
    copies = []

    def put(z, j, value):
        one[z, pl.ds(8 * j, 8), :] = value
        even = column_parity(8, columns) == z % 2
        zero = other_ref[z, pl.ds(8 * j, 8), :]
        low, high = jnp.where(even, zero, value), jnp.where(even, value, zero)
        for c in range(columns // LANES):
            at = slice(LANES * c, LANES * c + LANES)
            staged[z, c, pl.ds(2 * j, 8, stride=2 * tiles), :] = low[:, at]
            staged[z, c, pl.ds(2 * j + 1, 8, stride=2 * tiles), :] = high[:, at]
            if j == tiles - 1:
                copy = pltpu.make_async_copy(
                    staged.at[z, c], field_hbm.at[z, :, pl.ds(LANES * c, LANES)], sems.at[z, c]
                )
                copy.start()
                copies.append(copy)

    relax(where, own_ref, other_ref, charge_ref, ze_ref, zi_ref, xe_ref, xo_ref, 1, put)
    multipoles_of(1, lambda z, j: one[z, pl.ds(8 * j, 8), :], ((left0, radial0), (left1, radial1)), out_ref, right)
    for copy in copies:
        copy.wait()


def last_half_sweep(where, own, other, charge, halos, tables, after):
    planes, rows, columns = own.shape
    return pl.pallas_call(
        last_kernel,
        in_specs=[smem()] + [vmem()] * 11 + [anywhere()],
        out_specs=[hbm(), vmem()],
        out_shape=[shape_of(planes, 2 * rows, columns), sums_shape(planes)],
        scratch_shapes=[
            pltpu.VMEM(own.shape, jnp.float32),
            pltpu.VMEM((planes, columns // LANES, 2 * rows, LANES), jnp.float32),
            right_scratch(planes, columns),
            pltpu.SemaphoreType.DMA((planes, columns // LANES)),
        ],
        compiler_params=params(),
        cost_estimate=cost(100 * own.size, 0),
        name="relax_last",
    )(where, own, other, charge, *halos, *tables, after)


def swaps(pairs):
    return [(a, b) for a, b in pairs] + [(b, a) for a, b in pairs]


def odd_swaps(count):
    return swaps([(i, i + 1) for i in range(1, count - 1, 2)]) + [(0, 0), (count - 1, count - 1)]


def local(potential, regions, charge, levels):
    planes, row_count, columns = potential.shape
    gx, gz = lax.axis_index("gx"), lax.axis_index("gz")
    nx, nz = lax.axis_size("gx"), lax.axis_size("gz")
    rows_total = nx * row_count
    tiles = row_count // 16
    core = gz % 2
    where = jnp.stack(
        [core, gx % 2, jnp.where(core == 0, gz > 0, gz < nz - 1), gx > 0, gx < nx - 1, gx * row_count]
    ).astype(jnp.int32)
    start = where[5:]
    z_far, z_near = odd_swaps(nz), [(i, i ^ 1) for i in range(nz)]
    x_even, x_odd = [(i, i ^ 1) for i in range(nx)], odd_swaps(nx)

    def exchange(ze, zi, xe, xo):
        return (
            lax.ppermute(ze, "gz", z_far),
            lax.ppermute(zi, "gz", z_near),
            lax.ppermute(xe, "gx", x_even),
            lax.ppermute(xo, "gx", x_odd),
        )

    zero, one, charge0, charge1, *out = pack(where, potential, regions, charge, levels)
    after, tables = where, []
    for sweep in range(SWEEPS):
        halos = exchange(*out)
        zero, *out = half_sweep(where, zero, one, charge0, halos, 0, after)
        halos = exchange(*out)
        after = where
        if sweep < SWEEPS - 1:
            if sweep < 2:
                *table, after = angles(start, out[2], rows_total, tiles, columns, sweep)
                tables += table
            one, *out = half_sweep(where, one, zero, charge1, halos, 1, after)
            after = where
    sums0, after = multipole_sums(zero, tables)
    field, sums1 = last_half_sweep(where, one, zero, charge1, halos, tables, after)
    sums = (sums0 + sums1).reshape(planes, 2, TURNS, 2, STEPS, 8).sum(-1)
    cos_part = sums[:, 0, :, 0] - sums[:, 1, :, 1]
    sin_part = sums[:, 1, :, 0] + sums[:, 0, :, 1]
    part = jnp.concatenate([cos_part.reshape(planes, HALF), sin_part.reshape(planes, HALF)], axis=1)
    part = part * (1.0 / jnp.sqrt(jnp.float32(rows_total) * jnp.float32(columns)))
    share = K // nx
    part = jnp.transpose(part.reshape(planes, nx, share), (1, 0, 2))
    shares = lax.all_to_all(part, "gx", 0, 0, tiled=True)
    return field, jnp.sum(shares, axis=0)


def solution(mesh):
    in_specs = (P("gz", "gx", None), P("gz", "gx", None), P("gz", "gx", None), P())
    out_specs = (P("gz", "gx", None), P("gz", "gx"))
    return jax.shard_map(local, mesh=mesh, in_specs=in_specs, out_specs=out_specs, check_vma=False)
```

time: 569 us -> 133 us (0.23); the launches traced: 560 us -> 132 us
  other arithmetic: 200 us -> 0.99 us
  blocking collectives: 151 us -> 24.5 us
  waiting for transfers between devices: 65 us -> 10.1 us
  starting transfers between devices: 100 us -> 65.3 us
  matrix products: 27.3 us -> 0 us
  Pallas kernels: 0 us -> 23.8 us
  local copies, waits for them, and re-layouts: 15.4 us -> 6.29 us
    psum x1 -> x0, blocking collectives: 151 us -> none  [local(): summed = lax.psum(partial_terms, 'gx')]
    select_n x9 -> x0, other arithmetic: 134 us -> none  [the longest x8 116 us: relax_cells(): return jnp.where((free_cells > 0.5) & (parity_in == colour), moved, center)]
    mul x1 -> x0, other arithmetic: 63.7 us -> none  [make_basis(): radius * jnp.cos(orders * angle_grid)]
    ppermute x32, waiting for transfers between devices: 65 us -> 10.1 us  [the longest x8 6.53 us: exchange(): lax.ppermute(xe, 'gx', x_even)]
    ppermute x32, starting transfers between devices: 100 us -> 65.3 us  [the longest x8 37.2 us: exchange(): lax.ppermute(xe, 'gx', x_even)]
    dot_general x4 -> x0, matrix products: 27.3 us -> none  [local(): jnp.einsum('zxy,kxy->zk', field_now[:, start:start + block], basis_table,...]
    all_to_all x0 -> x1, blocking collectives: none -> 24.5 us  [local(): shares = lax.all_to_all(part, 'gx', 0, 0, tiled=True)]
    pallas_call x0 -> x12, Pallas kernels: none -> 23.8 us  [the longest x7 10.6 us: half_sweep(): pl.pallas_call(functools.partial(relax_kernel, colour), in_specs=[smem()]...]
  transfers between devices with their start and end apart: 32 -> 32, of which waited for: 29 -> 11; matrix products, arithmetic and copies ran while one was open for 12% -> 0% of each run, Pallas kernels for 0% -> 4%
where the time goes in v2:
time: 133 us; the launch traced here: 132 us
  starting transfers between devices  65.3 us (49%)
  blocking collectives  24.5 us (18%)
  Pallas kernels  23.8 us (18%)
  waiting for transfers between devices  10.1 us (8%)
  local copies, waits for them, and re-layouts  6.29 us (5%)
    ppermute x8, starting transfers between devices, exchange(): lax.ppermute(xe, 'gx', x_even)  37.2 us
    all_to_all x1, blocking collectives, local(): shares = lax.all_to_all(part, 'gx', 0, 0, tiled=True)  24.5 us
    ppermute x8, starting transfers between devices, exchange(): lax.ppermute(ze, 'gz', z_far)  18.1 us
    pallas_call x7, Pallas kernels, half_sweep(): pl.pallas_call(functools.partial(relax_kernel, colour), in_specs=[smem()]...  10.6 us
    ppermute x8, waiting for transfers between devices, exchange(): lax.ppermute(xe, 'gx', x_even)  6.53 us
    ppermute x8, starting transfers between devices, exchange(): lax.ppermute(xo, 'gx', x_odd)  5.42 us
    pallas_call x1, Pallas kernels, last_half_sweep(): pl.pallas_call(last_kernel, in_specs=[smem()] + [vmem()] * 11 + [anywhere...  4.96 us
    unnamed x6, local copies, waits for them, and re-layouts  4.77 us
  transfers between devices with their start and end apart: 32, of which 11 were waited for; matrix products, arithmetic and copies ran while one was open for 0% of the time, Pallas kernels for 4%

profile of v2, /device:TPU:8, one launch (start us, length us, event | category | flops | bytes accessed | tf_op | source)
XLA Modules:
  0.0 132.0 jit_solution(15544183337277998179)
XLA Ops:
  0.7 0.7 pad_bitcast_fusion.lev_ref
  1.4 1.6 %copy-done = f32[4,64,2048]{2,1,0:T(8,128)S(1)} copy-done((f32[4,64,2048]{2,1,0:T(8,128)S(1)}, f32[4,64,2048]{2,1,0:T(8,128)}, u32[]{:S(2)}) %copy-start) | copy-done | bytes 2097176
  3.0 1.6 %copy-done.1 = s32[4,64,2048]{2,1,0:T(8,128)S(1)} copy-done((s32[4,64,2048]{2,1,0:T(8,128)S(1)}, s32[4,64,2048]{2,1,0:T(8,128)}, u32[]{:S(2)}) %copy-start.1) | copy-done | bytes 2097176
  4.6 1.6 %copy-done.2 = f32[4,64,2048]{2,1,0:T(8,128)S(1)} copy-done((f32[4,64,2048]{2,1,0:T(8,128)S(1)}, f32[4,64,2048]{2,1,0:T(8,128)}, u32[]{:S(2)}) %copy-start.2) | copy-done | bytes 2097176
  6.2 3.1 %pack.1 = (f32[4,32,2048]{2,1,0:T(8,128)S(1)}, f32[4,32,2048]{2,1,0:T(8,128)S(1)}, f32[4,32,2048]{2,1,0:T(8,128)S(1)}, f32[4,32,2048]{2,1,0:T(8,128)S(1)}, f32[3...) custom-call(s32[6]{0:T(128)S(1)} %stack.39.where.after, ...), custom_call_target="tpu_custom_call" | custom-call | tf_op jit(solution)/shard_map/pack/pallas_call | solution.py:118
  9.3 1.9 %collective-permute-start = (f32[32,2048]{1,0:T(8,128)S(1)}, f32[32,2048]{1,0:T(8,128)S(1)}, u32[]{:S(2)}, u32[]{:S(2)}) collective-permute-start(f32[32,2048]{1,0:T(8,128)S(1)} %get-tuple-element.58), channel_id=1, source_target_pairs={{1,2},{3,4},{5,6},{2,1},{4,3},{6,5},{0,0},{7,7},{9,10},{11,12},{13... | collective-permute-start | bytes 786440 | tf_op jit(solution)/shard_map/ppermute | solution.py:382
  11.3 1.8 %collective-permute-start.1 = (f32[32,2048]{1,0:T(8,128)S(1)}, f32[32,2048]{1,0:T(8,128)S(1)}, u32[]{:S(2)}, u32[]{:S(2)}) collective-permute-start(f32[32,2048]{1,0:T(8,128)S(1)} %get-tuple-element.59), channel_id=1, source_target_pairs={{0,1},{1,0},{2,3},{3,2},{4,5},{5,4},{6,7},{7,6},{8,9},{9,8},{10,11... | collective-permute-start | bytes 786440 | tf_op jit(solution)/shard_map/ppermute | solution.py:383
  13.0 1.9 %collective-permute-start.2 = (f32[2,2048]{1,0:T(2,128)S(1)}, f32[2,2048]{1,0:T(2,128)S(1)}, u32[]{:S(2)}, u32[]{:S(2)}) collective-permute-start(f32[2,2048]{1,0:T(2,128)S(1)} %get-tuple-element.60), channel_id=1, source_target_pairs={{0,8},{8,0},{16,24},{24,16},{32,40},{40,32},{48,56},{56,48},{64,72... | collective-permute-start | bytes 49160 | tf_op jit(solution)/shard_map/ppermute | solution.py:384
  14.9 0.7 collective-permute-start.3
  15.6 1.2 collective-permute-done.2.xe_ref
  17.0 1.5 %relax.7 = (f32[4,32,2048]{2,1,0:T(8,128)S(1)}, f32[32,2048]{1,0:T(8,128)S(1)}, f32[32,2048]{1,0:T(8,128)S(1)}, f32[2,2048]{1,0:T(2,128)S(1)}, f32[2,2048]{1,0:T(2,128)S(1)}) custom-call(s32[6]{0:T(128)S(1)} %stack.39.where.after, f32[4,32,2048]{2,1,0:T(8,128)S(1)} %get-tuple-element.56.own_ref, f32[4,32,2048]{2,1,0:T(8,128)S(1)} %get-tuple-element.55.other_ref.own_ref, ...), custom_call_target="tpu_custom_call" | custom-call | flops 3670016 | tf_op jit(solution)/shard_map/relax/pallas_call | solution.py:189
  18.6 1.9 %collective-permute-start.4 = (f32[32,2048]{1,0:T(8,128)S(1)}, f32[32,2048]{1,0:T(8,128)S(1)}, u32[]{:S(2)}, u32[]{:S(2)}) collective-permute-start(f32[32,2048]{1,0:T(8,128)S(1)} %get-tuple-element.64), channel_id=1, source_target_pairs={{1,2},{3,4},{5,6},{2,1},{4,3},{6,5},{0,0},{7,7},{9,10},{11,12},{13... | collective-permute-start | bytes 786440 | tf_op jit(solution)/shard_map/ppermute | solution.py:382
  20.5 1.8 %collective-permute-start.5 = (f32[32,2048]{1,0:T(8,128)S(1)}, f32[32,2048]{1,0:T(8,128)S(1)}, u32[]{:S(2)}, u32[]{:S(2)}) collective-permute-start(f32[32,2048]{1,0:T(8,128)S(1)} %get-tuple-element.65), channel_id=1, source_target_pairs={{0,1},{1,0},{2,3},{3,2},{4,5},{5,4},{6,7},{7,6},{8,9},{9,8},{10,11... | collective-permute-start | bytes 786440 | tf_op jit(solution)/shard_map/ppermute | solution.py:383
  22.3 0.7 collective-permute-start.7
  22.9 8.4 %collective-permute-start.6 = (f32[2,2048]{1,0:T(2,128)S(1)}, f32[2,2048]{1,0:T(2,128)S(1)}, u32[]{:S(2)}, u32[]{:S(2)}) collective-permute-start(f32[2,2048]{1,0:T(2,128)S(1)} %get-tuple-element.66.after), channel_id=1, source_target_pairs={{0,8},{8,0},{16,24},{24,16},{32,40},{40,32},{48,56},{56,48},{64,72... | collective-permute-start | bytes 49160 | tf_op jit(solution)/shard_map/ppermute | solution.py:384
  31.3 1.3 angles.2
  33.1 1.5 %relax.8 = (f32[4,32,2048]{2,1,0:T(8,128)S(1)}, f32[32,2048]{1,0:T(8,128)S(1)}, f32[32,2048]{1,0:T(8,128)S(1)}, f32[2,2048]{1,0:T(2,128)S(1)}, f32[2,2048]{1,0:T(2,128)S(1)}) custom-call(s32[6]{0:T(128)S(1)} %stack.39.where.after, f32[4,32,2048]{2,1,0:T(8,128)S(1)} %get-tuple-element.55.other_ref.own_ref, ...), custom_call_target="tpu_custom_call" | custom-call | flops 3670016 | tf_op jit(solution)/shard_map/relax/pallas_call | solution.py:189
  34.6 1.9 %collective-permute-start.8 = (f32[32,2048]{1,0:T(8,128)S(1)}, f32[32,2048]{1,0:T(8,128)S(1)}, u32[]{:S(2)}, u32[]{:S(2)}) collective-permute-start(f32[32,2048]{1,0:T(8,128)S(1)} %get-tuple-element.70), channel_id=1, source_target_pairs={{1,2},{3,4},{5,6},{2,1},{4,3},{6,5},{0,0},{7,7},{9,10},{11,12},{13... | collective-permute-start | bytes 786440 | tf_op jit(solution)/shard_map/ppermute | solution.py:382
  36.9 2.0 %collective-permute-start.10 = (f32[2,2048]{1,0:T(2,128)S(1)}, f32[2,2048]{1,0:T(2,128)S(1)}, u32[]{:S(2)}, u32[]{:S(2)}) collective-permute-start(f32[2,2048]{1,0:T(2,128)S(1)} %get-tuple-element.72), channel_id=1, source_target_pairs={{0,8},{8,0},{16,24},{24,16},{32,40},{40,32},{48,56},{56,48},{64,72... | collective-permute-start | bytes 49160 | tf_op jit(solution)/shard_map/ppermute | solution.py:384
  38.9 0.7 collective-permute-start.11
  39.5 1.1 collective-permute-done.10.xe_ref
  40.6 1.7 %collective-permute-done.8.ze_ref = f32[32,2048]{1,0:T(8,128)S(1)} collective-permute-done((f32[32,2048]{1,0:T(8,128)S(1)}, f32[32,2048]{1,0:T(8,128)S(1)}, u32[]{:S(2)}, u32[]{:S(2)}) %collective-permute-start.8) | collective-permute-done | bytes 262176 | tf_op jit(solution)/shard_map/ppermute | solution.py:382
  42.3 1.5 %relax.9 = (f32[4,32,2048]{2,1,0:T(8,128)S(1)}, f32[32,2048]{1,0:T(8,128)S(1)}, f32[32,2048]{1,0:T(8,128)S(1)}, f32[2,2048]{1,0:T(2,128)S(1)}, f32[2,2048]{1,0:T(2,128)S(1)}) custom-call(s32[6]{0:T(128)S(1)} %stack.39.where.after, f32[4,32,2048]{2,1,0:T(8,128)S(1)} %get-tuple-element.62.other_ref.own_ref, ...), custom_call_target="tpu_custom_call" | custom-call | flops 3670016 | tf_op jit(solution)/shard_map/relax/pallas_call | solution.py:189
  43.8 1.9 %collective-permute-start.12 = (f32[32,2048]{1,0:T(8,128)S(1)}, f32[32,2048]{1,0:T(8,128)S(1)}, u32[]{:S(2)}, u32[]{:S(2)}) collective-permute-start(f32[32,2048]{1,0:T(8,128)S(1)} %get-tuple-element.75), channel_id=1, source_target_pairs={{1,2},{3,4},{5,6},{2,1},{4,3},{6,5},{0,0},{7,7},{9,10},{11,12},{13... | collective-permute-start | bytes 786440 | tf_op jit(solution)/shard_map/ppermute | solution.py:382
  46.1 0.7 collective-permute-start.15
  46.7 9.0 %collective-permute-start.14 = (f32[2,2048]{1,0:T(2,128)S(1)}, f32[2,2048]{1,0:T(2,128)S(1)}, u32[]{:S(2)}, u32[]{:S(2)}) collective-permute-start(f32[2,2048]{1,0:T(2,128)S(1)} %get-tuple-element.77.after), channel_id=1, source_target_pairs={{0,8},{8,0},{16,24},{24,16},{32,40},{40,32},{48,56},{56,48},{64,72... | collective-permute-start | bytes 49160 | tf_op jit(solution)/shard_map/ppermute | solution.py:384
  55.7 1.3 angles.3
  57.5 1.5 %relax.10 = (f32[4,32,2048]{2,1,0:T(8,128)S(1)}, f32[32,2048]{1,0:T(8,128)S(1)}, f32[32,2048]{1,0:T(8,128)S(1)}, f32[2,2048]{1,0:T(2,128)S(1)}, f32[2,2048]{1,0:T(2,128)S(1)}) custom-call(s32[6]{0:T(128)S(1)} %stack.39.where.after, f32[4,32,2048]{2,1,0:T(8,128)S(1)} %get-tuple-element.69.other_ref.own_ref, ...), custom_call_target="tpu_custom_call" | custom-call | flops 3670016 | tf_op jit(solution)/shard_map/relax/pallas_call | solution.py:189
  59.0 2.5 %collective-permute-start.16 = (f32[32,2048]{1,0:T(8,128)S(1)}, f32[32,2048]{1,0:T(8,128)S(1)}, u32[]{:S(2)}, u32[]{:S(2)}) collective-permute-start(f32[32,2048]{1,0:T(8,128)S(1)} %get-tuple-element.81), channel_id=1, source_target_pairs={{1,2},{3,4},{5,6},{2,1},{4,3},{6,5},{0,0},{7,7},{9,10},{11,12},{13... | collective-permute-start | bytes 786440 | tf_op jit(solution)/shard_map/ppermute | solution.py:382
  61.6 1.9 %collective-permute-start.18 = (f32[2,2048]{1,0:T(2,128)S(1)}, f32[2,2048]{1,0:T(2,128)S(1)}, u32[]{:S(2)}, u32[]{:S(2)}) collective-permute-start(f32[2,2048]{1,0:T(2,128)S(1)} %get-tuple-element.83), channel_id=1, source_target_pairs={{0,8},{8,0},{16,24},{24,16},{32,40},{40,32},{48,56},{56,48},{64,72... | collective-permute-start | bytes 49160 | tf_op jit(solution)/shard_map/ppermute | solution.py:384
  63.5 0.7 collective-permute-start.19
  64.1 1.3 collective-permute-done.18.xe_ref
  65.5 1.2 collective-permute-done.16.ze_ref
  66.7 1.5 %relax.11 = (f32[4,32,2048]{2,1,0:T(8,128)S(1)}, f32[32,2048]{1,0:T(8,128)S(1)}, f32[32,2048]{1,0:T(8,128)S(1)}, f32[2,2048]{1,0:T(2,128)S(1)}, f32[2,2048]{1,0:T(2,128)S(1)}) custom-call(s32[6]{0:T(128)S(1)} %stack.39.where.after, f32[4,32,2048]{2,1,0:T(8,128)S(1)} %get-tuple-element.74.other_ref.own_ref, ...), custom_call_target="tpu_custom_call" | custom-call | flops 3670016 | tf_op jit(solution)/shard_map/relax/pallas_call | solution.py:189
  68.2 2.5 %collective-permute-start.20 = (f32[32,2048]{1,0:T(8,128)S(1)}, f32[32,2048]{1,0:T(8,128)S(1)}, u32[]{:S(2)}, u32[]{:S(2)}) collective-permute-start(f32[32,2048]{1,0:T(8,128)S(1)} %get-tuple-element.86), channel_id=1, source_target_pairs={{1,2},{3,4},{5,6},{2,1},{4,3},{6,5},{0,0},{7,7},{9,10},{11,12},{13... | collective-permute-start | bytes 786440 | tf_op jit(solution)/shard_map/ppermute | solution.py:382
  70.8 2.9 %collective-permute-start.22 = (f32[2,2048]{1,0:T(2,128)S(1)}, f32[2,2048]{1,0:T(2,128)S(1)}, u32[]{:S(2)}, u32[]{:S(2)}) collective-permute-start(f32[2,2048]{1,0:T(2,128)S(1)} %get-tuple-element.88), channel_id=1, source_target_pairs={{0,8},{8,0},{16,24},{24,16},{32,40},{40,32},{48,56},{56,48},{64,72... | collective-permute-start | bytes 49160 | tf_op jit(solution)/shard_map/ppermute | solution.py:384
  74.4 1.1 collective-permute-done.22.xe_ref
  75.9 1.5 %relax.12 = (f32[4,32,2048]{2,1,0:T(8,128)S(1)}, f32[32,2048]{1,0:T(8,128)S(1)}, f32[32,2048]{1,0:T(8,128)S(1)}, f32[2,2048]{1,0:T(2,128)S(1)}, f32[2,2048]{1,0:T(2,128)S(1)}) custom-call(s32[6]{0:T(128)S(1)} %stack.39.where.after, f32[4,32,2048]{2,1,0:T(8,128)S(1)} %get-tuple-element.80.other_ref.own_ref, ...), custom_call_target="tpu_custom_call" | custom-call | flops 3670016 | tf_op jit(solution)/shard_map/relax/pallas_call | solution.py:189
  77.4 2.8 %collective-permute-start.24 = (f32[32,2048]{1,0:T(8,128)S(1)}, f32[32,2048]{1,0:T(8,128)S(1)}, u32[]{:S(2)}, u32[]{:S(2)}) collective-permute-start(f32[32,2048]{1,0:T(8,128)S(1)} %get-tuple-element.91), channel_id=1, source_target_pairs={{1,2},{3,4},{5,6},{2,1},{4,3},{6,5},{0,0},{7,7},{9,10},{11,12},{13... | collective-permute-start | bytes 786440 | tf_op jit(solution)/shard_map/ppermute | solution.py:382
  80.4 4.5 %collective-permute-start.26 = (f32[2,2048]{1,0:T(2,128)S(1)}, f32[2,2048]{1,0:T(2,128)S(1)}, u32[]{:S(2)}, u32[]{:S(2)}) collective-permute-start(f32[2,2048]{1,0:T(2,128)S(1)} %get-tuple-element.93), channel_id=1, source_target_pairs={{0,8},{8,0},{16,24},{24,16},{32,40},{40,32},{48,56},{56,48},{64,72... | collective-permute-start | bytes 49160 | tf_op jit(solution)/shard_map/ppermute | solution.py:384
  85.6 1.1 collective-permute-done.26.xe_ref
  86.6 1.5 %relax.13 = (f32[4,32,2048]{2,1,0:T(8,128)S(1)}, f32[32,2048]{1,0:T(8,128)S(1)}, f32[32,2048]{1,0:T(8,128)S(1)}, f32[2,2048]{1,0:T(2,128)S(1)}, f32[2,2048]{1,0:T(2,128)S(1)}) custom-call(s32[6]{0:T(128)S(1)} %stack.39.where.after, f32[4,32,2048]{2,1,0:T(8,128)S(1)} %get-tuple-element.85.other_ref.own_ref, ...), custom_call_target="tpu_custom_call" | custom-call | flops 3670016 | tf_op jit(solution)/shard_map/relax/pallas_call | solution.py:189
  88.2 2.5 %collective-permute-start.28 = (f32[32,2048]{1,0:T(8,128)S(1)}, f32[32,2048]{1,0:T(8,128)S(1)}, u32[]{:S(2)}, u32[]{:S(2)}) collective-permute-start(f32[32,2048]{1,0:T(8,128)S(1)} %get-tuple-element.96), channel_id=1, source_target_pairs={{1,2},{3,4},{5,6},{2,1},{4,3},{6,5},{0,0},{7,7},{9,10},{11,12},{13... | collective-permute-start | bytes 786440 | tf_op jit(solution)/shard_map/ppermute | solution.py:382
  90.8 6.5 %collective-permute-start.30 = (f32[2,2048]{1,0:T(2,128)S(1)}, f32[2,2048]{1,0:T(2,128)S(1)}, u32[]{:S(2)}, u32[]{:S(2)}) collective-permute-start(f32[2,2048]{1,0:T(2,128)S(1)} %get-tuple-element.98), channel_id=1, source_target_pairs={{0,8},{8,0},{16,24},{24,16},{32,40},{40,32},{48,56},{56,48},{64,72... | collective-permute-start | bytes 49160 | tf_op jit(solution)/shard_map/ppermute | solution.py:384
  97.3 0.9 collective-permute-start.31
  98.2 2.5 %multipole.1 = (f32[4,16,64]{2,1,0:T(8,128)S(1)}, f32[8,128]{1,0:T(8,128)S(1)}) custom-call(f32[4,32,2048]{2,1,0:T(8,128)S(1)} %get-tuple-element.95.field_ref.other_ref, bf16[4,256,2048]{2,1,0:T(8,128)(2,1)S(1)} %get-tuple-element.100.left0, f32[4,64,2048]{2,1,0:T(8,128)S(1)} %get-tuple-element.101.radial0, ...), custom_call_target="tpu_custom_call" | custom-call | flops 26214400 | tf_op jit(solution)/shard_map/multipole/pallas_call | solution.py:298
  100.7 5.0 %relax_last.1 = (f32[4,64,2048]{2,1,0:T(8,128)}, f32[4,16,64]{2,1,0:T(8,128)S(1)}) custom-call(s32[6]{0:T(128)S(1)} %stack.39.where.after, f32[4,32,2048]{2,1,0:T(8,128)S(1)} %get-tuple-element.90.other_ref.own_ref, f32[4,32,2048]{2,1,0:T(8,128)S(1)} %get-tuple-element.95.field_ref.other_ref, f32[4,32,2048]{2,1,0:T(8,128)S(1)} %get-tuple-element.63.charge_ref, ...), custom_call_target="tpu_custom_call" | custom-call | flops 26214400 | tf_op jit(solution)/shard_map/relax_last/pallas_call | solution.py:341
  106.9 24.5 %all_to_all.5 = f32[32,4,2]{1,2,0:T(2,128)S(1)} all-to-all(f32[32,4,2]{1,2,0:T(2,128)S(1)} %copy.20), channel_id=1, replica_groups=mesh['gx'=32,'gz'=8] {'gx'}, dimensions={0} | all-to-all | bytes 2048 | tf_op jit(solution)/shard_map/all_to_all | solution.py:410
  (48 shorter events, 5.8 us)
Async XLA Ops:
  1.4 1.6 %copy-start = (f32[4,64,2048]{2,1,0:T(8,128)S(1)}, f32[4,64,2048]{2,1,0:T(8,128)}, u32[]{:S(2)}) copy-start(f32[4,64,2048]{2,1,0:T(8,128)} %pot_hbm.1) | copy-start | bytes 6291460
  3.0 1.6 %copy-start.1 = (s32[4,64,2048]{2,1,0:T(8,128)S(1)}, s32[4,64,2048]{2,1,0:T(8,128)}, u32[]{:S(2)}) copy-start(s32[4,64,2048]{2,1,0:T(8,128)} %reg_hbm.1) | copy-start | bytes 6291460
  4.6 1.6 %copy-start.2 = (f32[4,64,2048]{2,1,0:T(8,128)S(1)}, f32[4,64,2048]{2,1,0:T(8,128)}, u32[]{:S(2)}) copy-start(f32[4,64,2048]{2,1,0:T(8,128)} %chg_hbm.1) | copy-start | bytes 6291460
  9.3 7.7 %collective-permute-start = (f32[32,2048]{1,0:T(8,128)S(1)}, f32[32,2048]{1,0:T(8,128)S(1)}, u32[]{:S(2)}, u32[]{:S(2)}) collective-permute-start(f32[32,2048]{1,0:T(8,128)S(1)} %get-tuple-element.58), channel_id=1, source_target_pairs={{1,2},{3,4},{5,6},{2,1},{4,3},{6,5},{0,0},{7,7},{9,10},{11,12},{13... | collective-permute-start | bytes 786440 | tf_op jit(solution)/shard_map/ppermute | solution.py:382
  11.3 5.8 %collective-permute-start.1 = (f32[32,2048]{1,0:T(8,128)S(1)}, f32[32,2048]{1,0:T(8,128)S(1)}, u32[]{:S(2)}, u32[]{:S(2)}) collective-permute-start(f32[32,2048]{1,0:T(8,128)S(1)} %get-tuple-element.59), channel_id=1, source_target_pairs={{0,1},{1,0},{2,3},{3,2},{4,5},{5,4},{6,7},{7,6},{8,9},{9,8},{10,11... | collective-permute-start | bytes 786440 | tf_op jit(solution)/shard_map/ppermute | solution.py:383
  13.0 3.7 %collective-permute-start.2 = (f32[2,2048]{1,0:T(2,128)S(1)}, f32[2,2048]{1,0:T(2,128)S(1)}, u32[]{:S(2)}, u32[]{:S(2)}) collective-permute-start(f32[2,2048]{1,0:T(2,128)S(1)} %get-tuple-element.60), channel_id=1, source_target_pairs={{0,8},{8,0},{16,24},{24,16},{32,40},{40,32},{48,56},{56,48},{64,72... | collective-permute-start | bytes 49160 | tf_op jit(solution)/shard_map/ppermute | solution.py:384
  14.9 1.8 %collective-permute-start.3 = (f32[2,2048]{1,0:T(2,128)S(1)}, f32[2,2048]{1,0:T(2,128)S(1)}, u32[]{:S(2)}, u32[]{:S(2)}) collective-permute-start(f32[2,2048]{1,0:T(2,128)S(1)} %get-tuple-element.61), channel_id=1, source_target_pairs={{8,16},{24,32},{40,48},{56,64},{72,80},{88,96},{104,112},{120,128}... | collective-permute-start | bytes 49160 | tf_op jit(solution)/shard_map/ppermute | solution.py:385
  18.6 14.5 %collective-permute-start.4 = (f32[32,2048]{1,0:T(8,128)S(1)}, f32[32,2048]{1,0:T(8,128)S(1)}, u32[]{:S(2)}, u32[]{:S(2)}) collective-permute-start(f32[32,2048]{1,0:T(8,128)S(1)} %get-tuple-element.64), channel_id=1, source_target_pairs={{1,2},{3,4},{5,6},{2,1},{4,3},{6,5},{0,0},{7,7},{9,10},{11,12},{13... | collective-permute-start | bytes 786440 | tf_op jit(solution)/shard_map/ppermute | solution.py:382
  20.5 12.6 %collective-permute-start.5 = (f32[32,2048]{1,0:T(8,128)S(1)}, f32[32,2048]{1,0:T(8,128)S(1)}, u32[]{:S(2)}, u32[]{:S(2)}) collective-permute-start(f32[32,2048]{1,0:T(8,128)S(1)} %get-tuple-element.65), channel_id=1, source_target_pairs={{0,1},{1,0},{2,3},{3,2},{4,5},{5,4},{6,7},{7,6},{8,9},{9,8},{10,11... | collective-permute-start | bytes 786440 | tf_op jit(solution)/shard_map/ppermute | solution.py:383
  22.3 10.3 %collective-permute-start.7 = (f32[2,2048]{1,0:T(2,128)S(1)}, f32[2,2048]{1,0:T(2,128)S(1)}, u32[]{:S(2)}, u32[]{:S(2)}) collective-permute-start(f32[2,2048]{1,0:T(2,128)S(1)} %get-tuple-element.67), channel_id=1, source_target_pairs={{8,16},{24,32},{40,48},{56,64},{72,80},{88,96},{104,112},{120,128}... | collective-permute-start | bytes 49160 | tf_op jit(solution)/shard_map/ppermute | solution.py:385
  22.9 10.1 %collective-permute-start.6 = (f32[2,2048]{1,0:T(2,128)S(1)}, f32[2,2048]{1,0:T(2,128)S(1)}, u32[]{:S(2)}, u32[]{:S(2)}) collective-permute-start(f32[2,2048]{1,0:T(2,128)S(1)} %get-tuple-element.66.after), channel_id=1, source_target_pairs={{0,8},{8,0},{16,24},{24,16},{32,40},{40,32},{48,56},{56,48},{64,72... | collective-permute-start | bytes 49160 | tf_op jit(solution)/shard_map/ppermute | solution.py:384
  34.6 7.7 %collective-permute-start.8 = (f32[32,2048]{1,0:T(8,128)S(1)}, f32[32,2048]{1,0:T(8,128)S(1)}, u32[]{:S(2)}, u32[]{:S(2)}) collective-permute-start(f32[32,2048]{1,0:T(8,128)S(1)} %get-tuple-element.70), channel_id=1, source_target_pairs={{1,2},{3,4},{5,6},{2,1},{4,3},{6,5},{0,0},{7,7},{9,10},{11,12},{13... | collective-permute-start | bytes 786440 | tf_op jit(solution)/shard_map/ppermute | solution.py:382
  36.5 5.8 %collective-permute-start.9 = (f32[32,2048]{1,0:T(8,128)S(1)}, f32[32,2048]{1,0:T(8,128)S(1)}, u32[]{:S(2)}, u32[]{:S(2)}) collective-permute-start(f32[32,2048]{1,0:T(8,128)S(1)} %get-tuple-element.71), channel_id=1, source_target_pairs={{0,1},{1,0},{2,3},{3,2},{4,5},{5,4},{6,7},{7,6},{8,9},{9,8},{10,11... | collective-permute-start | bytes 786440 | tf_op jit(solution)/shard_map/ppermute | solution.py:383
  36.9 3.7 %collective-permute-start.10 = (f32[2,2048]{1,0:T(2,128)S(1)}, f32[2,2048]{1,0:T(2,128)S(1)}, u32[]{:S(2)}, u32[]{:S(2)}) collective-permute-start(f32[2,2048]{1,0:T(2,128)S(1)} %get-tuple-element.72), channel_id=1, source_target_pairs={{0,8},{8,0},{16,24},{24,16},{32,40},{40,32},{48,56},{56,48},{64,72... | collective-permute-start | bytes 49160 | tf_op jit(solution)/shard_map/ppermute | solution.py:384
  38.9 1.7 %collective-permute-start.11 = (f32[2,2048]{1,0:T(2,128)S(1)}, f32[2,2048]{1,0:T(2,128)S(1)}, u32[]{:S(2)}, u32[]{:S(2)}) collective-permute-start(f32[2,2048]{1,0:T(2,128)S(1)} %get-tuple-element.73), channel_id=1, source_target_pairs={{8,16},{24,32},{40,48},{56,64},{72,80},{88,96},{104,112},{120,128}... | collective-permute-start | bytes 49160 | tf_op jit(solution)/shard_map/ppermute | solution.py:385
  43.8 13.7 %collective-permute-start.12 = (f32[32,2048]{1,0:T(8,128)S(1)}, f32[32,2048]{1,0:T(8,128)S(1)}, u32[]{:S(2)}, u32[]{:S(2)}) collective-permute-start(f32[32,2048]{1,0:T(8,128)S(1)} %get-tuple-element.75), channel_id=1, source_target_pairs={{1,2},{3,4},{5,6},{2,1},{4,3},{6,5},{0,0},{7,7},{9,10},{11,12},{13... | collective-permute-start | bytes 786440 | tf_op jit(solution)/shard_map/ppermute | solution.py:382
  45.7 11.7 %collective-permute-start.13 = (f32[32,2048]{1,0:T(8,128)S(1)}, f32[32,2048]{1,0:T(8,128)S(1)}, u32[]{:S(2)}, u32[]{:S(2)}) collective-permute-start(f32[32,2048]{1,0:T(8,128)S(1)} %get-tuple-element.76), channel_id=1, source_target_pairs={{0,1},{1,0},{2,3},{3,2},{4,5},{5,4},{6,7},{7,6},{8,9},{9,8},{10,11... | collective-permute-start | bytes 786440 | tf_op jit(solution)/shard_map/ppermute | solution.py:383
  46.1 10.9 %collective-permute-start.15 = (f32[2,2048]{1,0:T(2,128)S(1)}, f32[2,2048]{1,0:T(2,128)S(1)}, u32[]{:S(2)}, u32[]{:S(2)}) collective-permute-start(f32[2,2048]{1,0:T(2,128)S(1)} %get-tuple-element.78), channel_id=1, source_target_pairs={{8,16},{24,32},{40,48},{56,64},{72,80},{88,96},{104,112},{120,128}... | collective-permute-start | bytes 49160 | tf_op jit(solution)/shard_map/ppermute | solution.py:385
  46.7 10.7 %collective-permute-start.14 = (f32[2,2048]{1,0:T(2,128)S(1)}, f32[2,2048]{1,0:T(2,128)S(1)}, u32[]{:S(2)}, u32[]{:S(2)}) collective-permute-start(f32[2,2048]{1,0:T(2,128)S(1)} %get-tuple-element.77.after), channel_id=1, source_target_pairs={{0,8},{8,0},{16,24},{24,16},{32,40},{40,32},{48,56},{56,48},{64,72... | collective-permute-start | bytes 49160 | tf_op jit(solution)/shard_map/ppermute | solution.py:384
  59.0 7.7 %collective-permute-start.16 = (f32[32,2048]{1,0:T(8,128)S(1)}, f32[32,2048]{1,0:T(8,128)S(1)}, u32[]{:S(2)}, u32[]{:S(2)}) collective-permute-start(f32[32,2048]{1,0:T(8,128)S(1)} %get-tuple-element.81), channel_id=1, source_target_pairs={{1,2},{3,4},{5,6},{2,1},{4,3},{6,5},{0,0},{7,7},{9,10},{11,12},{13... | collective-permute-start | bytes 786440 | tf_op jit(solution)/shard_map/ppermute | solution.py:382
  61.5 5.1 %collective-permute-start.17 = (f32[32,2048]{1,0:T(8,128)S(1)}, f32[32,2048]{1,0:T(8,128)S(1)}, u32[]{:S(2)}, u32[]{:S(2)}) collective-permute-start(f32[32,2048]{1,0:T(8,128)S(1)} %get-tuple-element.82), channel_id=1, source_target_pairs={{0,1},{1,0},{2,3},{3,2},{4,5},{5,4},{6,7},{7,6},{8,9},{9,8},{10,11... | collective-permute-start | bytes 786440 | tf_op jit(solution)/shard_map/ppermute | solution.py:383
  61.6 3.8 %collective-permute-start.18 = (f32[2,2048]{1,0:T(2,128)S(1)}, f32[2,2048]{1,0:T(2,128)S(1)}, u32[]{:S(2)}, u32[]{:S(2)}) collective-permute-start(f32[2,2048]{1,0:T(2,128)S(1)} %get-tuple-element.83), channel_id=1, source_target_pairs={{0,8},{8,0},{16,24},{24,16},{32,40},{40,32},{48,56},{56,48},{64,72... | collective-permute-start | bytes 49160 | tf_op jit(solution)/shard_map/ppermute | solution.py:384
  63.5 2.0 %collective-permute-start.19 = (f32[2,2048]{1,0:T(2,128)S(1)}, f32[2,2048]{1,0:T(2,128)S(1)}, u32[]{:S(2)}, u32[]{:S(2)}) collective-permute-start(f32[2,2048]{1,0:T(2,128)S(1)} %get-tuple-element.84), channel_id=1, source_target_pairs={{8,16},{24,32},{40,48},{56,64},{72,80},{88,96},{104,112},{120,128}... | collective-permute-start | bytes 49160 | tf_op jit(solution)/shard_map/ppermute | solution.py:385
  68.2 7.7 %collective-permute-start.20 = (f32[32,2048]{1,0:T(8,128)S(1)}, f32[32,2048]{1,0:T(8,128)S(1)}, u32[]{:S(2)}, u32[]{:S(2)}) collective-permute-start(f32[32,2048]{1,0:T(8,128)S(1)} %get-tuple-element.86), channel_id=1, source_target_pairs={{1,2},{3,4},{5,6},{2,1},{4,3},{6,5},{0,0},{7,7},{9,10},{11,12},{13... | collective-permute-start | bytes 786440 | tf_op jit(solution)/shard_map/ppermute | solution.py:382
  70.7 5.1 %collective-permute-start.21 = (f32[32,2048]{1,0:T(8,128)S(1)}, f32[32,2048]{1,0:T(8,128)S(1)}, u32[]{:S(2)}, u32[]{:S(2)}) collective-permute-start(f32[32,2048]{1,0:T(8,128)S(1)} %get-tuple-element.87), channel_id=1, source_target_pairs={{0,1},{1,0},{2,3},{3,2},{4,5},{5,4},{6,7},{7,6},{8,9},{9,8},{10,11... | collective-permute-start | bytes 786440 | tf_op jit(solution)/shard_map/ppermute | solution.py:383
  70.8 4.6 %collective-permute-start.22 = (f32[2,2048]{1,0:T(2,128)S(1)}, f32[2,2048]{1,0:T(2,128)S(1)}, u32[]{:S(2)}, u32[]{:S(2)}) collective-permute-start(f32[2,2048]{1,0:T(2,128)S(1)} %get-tuple-element.88), channel_id=1, source_target_pairs={{0,8},{8,0},{16,24},{24,16},{32,40},{40,32},{48,56},{56,48},{64,72... | collective-permute-start | bytes 49160 | tf_op jit(solution)/shard_map/ppermute | solution.py:384
  73.8 1.7 %collective-permute-start.23 = (f32[2,2048]{1,0:T(2,128)S(1)}, f32[2,2048]{1,0:T(2,128)S(1)}, u32[]{:S(2)}, u32[]{:S(2)}) collective-permute-start(f32[2,2048]{1,0:T(2,128)S(1)} %get-tuple-element.89), channel_id=1, source_target_pairs={{8,16},{24,32},{40,48},{56,64},{72,80},{88,96},{104,112},{120,128}... | collective-permute-start | bytes 49160 | tf_op jit(solution)/shard_map/ppermute | solution.py:385
  77.4 9.2 %collective-permute-start.24 = (f32[32,2048]{1,0:T(8,128)S(1)}, f32[32,2048]{1,0:T(8,128)S(1)}, u32[]{:S(2)}, u32[]{:S(2)}) collective-permute-start(f32[32,2048]{1,0:T(8,128)S(1)} %get-tuple-element.91), channel_id=1, source_target_pairs={{1,2},{3,4},{5,6},{2,1},{4,3},{6,5},{0,0},{7,7},{9,10},{11,12},{13... | collective-permute-start | bytes 786440 | tf_op jit(solution)/shard_map/ppermute | solution.py:382
  80.3 6.4 %collective-permute-start.25 = (f32[32,2048]{1,0:T(8,128)S(1)}, f32[32,2048]{1,0:T(8,128)S(1)}, u32[]{:S(2)}, u32[]{:S(2)}) collective-permute-start(f32[32,2048]{1,0:T(8,128)S(1)} %get-tuple-element.92), channel_id=1, source_target_pairs={{0,1},{1,0},{2,3},{3,2},{4,5},{5,4},{6,7},{7,6},{8,9},{9,8},{10,11... | collective-permute-start | bytes 786440 | tf_op jit(solution)/shard_map/ppermute | solution.py:383
  80.4 6.3 %collective-permute-start.26 = (f32[2,2048]{1,0:T(2,128)S(1)}, f32[2,2048]{1,0:T(2,128)S(1)}, u32[]{:S(2)}, u32[]{:S(2)}) collective-permute-start(f32[2,2048]{1,0:T(2,128)S(1)} %get-tuple-element.93), channel_id=1, source_target_pairs={{0,8},{8,0},{16,24},{24,16},{32,40},{40,32},{48,56},{56,48},{64,72... | collective-permute-start | bytes 49160 | tf_op jit(solution)/shard_map/ppermute | solution.py:384
  84.9 1.7 %collective-permute-start.27 = (f32[2,2048]{1,0:T(2,128)S(1)}, f32[2,2048]{1,0:T(2,128)S(1)}, u32[]{:S(2)}, u32[]{:S(2)}) collective-permute-start(f32[2,2048]{1,0:T(2,128)S(1)} %get-tuple-element.94), channel_id=1, source_target_pairs={{8,16},{24,32},{40,48},{56,64},{72,80},{88,96},{104,112},{120,128}... | collective-permute-start | bytes 49160 | tf_op jit(solution)/shard_map/ppermute | solution.py:385
  88.2 12.5 %collective-permute-start.28 = (f32[32,2048]{1,0:T(8,128)S(1)}, f32[32,2048]{1,0:T(8,128)S(1)}, u32[]{:S(2)}, u32[]{:S(2)}) collective-permute-start(f32[32,2048]{1,0:T(8,128)S(1)} %get-tuple-element.96), channel_id=1, source_target_pairs={{1,2},{3,4},{5,6},{2,1},{4,3},{6,5},{0,0},{7,7},{9,10},{11,12},{13... | collective-permute-start | bytes 786440 | tf_op jit(solution)/shard_map/ppermute | solution.py:382
  90.7 10.0 %collective-permute-start.29 = (f32[32,2048]{1,0:T(8,128)S(1)}, f32[32,2048]{1,0:T(8,128)S(1)}, u32[]{:S(2)}, u32[]{:S(2)}) collective-permute-start(f32[32,2048]{1,0:T(8,128)S(1)} %get-tuple-element.97), channel_id=1, source_target_pairs={{0,1},{1,0},{2,3},{3,2},{4,5},{5,4},{6,7},{7,6},{8,9},{9,8},{10,11... | collective-permute-start | bytes 786440 | tf_op jit(solution)/shard_map/ppermute | solution.py:383
  90.8 9.9 %collective-permute-start.30 = (f32[2,2048]{1,0:T(2,128)S(1)}, f32[2,2048]{1,0:T(2,128)S(1)}, u32[]{:S(2)}, u32[]{:S(2)}) collective-permute-start(f32[2,2048]{1,0:T(2,128)S(1)} %get-tuple-element.98), channel_id=1, source_target_pairs={{0,8},{8,0},{16,24},{24,16},{32,40},{40,32},{48,56},{56,48},{64,72... | collective-permute-start | bytes 49160 | tf_op jit(solution)/shard_map/ppermute | solution.py:384
  97.3 3.4 %collective-permute-start.31 = (f32[2,2048]{1,0:T(2,128)S(1)}, f32[2,2048]{1,0:T(2,128)S(1)}, u32[]{:S(2)}, u32[]{:S(2)}) collective-permute-start(f32[2,2048]{1,0:T(2,128)S(1)} %get-tuple-element.99), channel_id=1, source_target_pairs={{8,16},{24,32},{40,48},{56,64},{72,80},{88,96},{104,112},{120,128}... | collective-permute-start | bytes 49160 | tf_op jit(solution)/shard_map/ppermute | solution.py:385
